TPU v7x, 512 devices: a whole 4x8x8 slice. The times are simulated.
512 devices in a mesh: gx: 32 (over y, x_lo, core), gy: 16 (over x_hi, z).
Axes of the slice: x: 4 (x_hi: 2, x_lo: 2; x = x_hi * 2 + x_lo), y: 8, z: 8, core: 2. Of those that a mesh axis runs over, the one named last changes fastest.
Arguments:
- obstacles: int32 [4096, 4096], P('gx', 'gy'), may hold values 0 or 1
- load: float32 [4096, 4096], P('gx', 'gy'), may hold values from 0.25 to 4
- exit_rows: int32 [4, 4096], replicated, may hold values from 0 to 4095
- exit_cols: int32 [4, 4096], replicated, may hold values from 0 to 4095
Outputs:
- potential: float32 [4, 4096, 4096], P(None, 'gx', 'gy')
All inputs are finite; a program needn't handle non-finite values. No bound on the sum of `obstacles` on one device may be relied on, other than what follows from the above.
Results may differ from a plain program's by a relative error of at most 0.0001.
Values sent between devices are 32-bit elements; how exact they have to be, the bound alone decides.
No kernel may reach another device: no remote copies, remote signals or barrier semaphores. Data moves between devices by JAX's collectives and lax.ppermute only.
A program may use at most 64 MiB of HBM per device.

v0:
```python
import jax
import jax.numpy as jnp
from jax import lax
from jax.sharding import PartitionSpec as P

COARSEN = 4
SMOOTH = 4
CSWEEPS = 4


SCREENING = 0.0001
EXIT_SINK = 4.0
COARSE_SHIFT = 0.01
DAMPING = 0.8
UPPER_BOUND = 12.5
LOWER_BOUND = 1.0


def with_halo(x, sides, width):
    for axis, dim in sides:
        peers, length = (lax.axis_size(axis), x.shape[dim])
        up = [(i, (i + 1) % peers) for i in range(peers - 1)]
        down = [(j, i) for i, j in up]
        last = lax.slice_in_dim(x, length - width, length, axis=dim)
        initial = lax.slice_in_dim(x, 0, width, axis=dim)
        before = lax.ppermute(last, axis, up)
        after = lax.ppermute(initial, axis, down)
        x = jnp.concatenate([before, x, after], axis=dim)
    return x


def with_halo_2(x, sides, width):
    edges = {}
    for axis, dim in sides:
        peers, length = (lax.axis_size(axis), x.shape[dim])
        up = [(i, (i + 1) % peers) for i in range(peers - 1)]
        last = lax.slice_in_dim(x, length - width, length, axis=dim)
        initial = lax.slice_in_dim(x, 0, width, axis=dim)
        edges[dim] = (
            lax.ppermute(last, axis, up),
            lax.ppermute(initial, axis, [(b, a) for a, b in up]),
        )
    done = []
    for _, dim in sides:
        low, high = edges[dim]
        around = [(width, width) if d in done else (0, 0) for d in range(x.ndim)]
        x = jnp.concatenate([jnp.pad(low, around), x, jnp.pad(high, around)], axis=dim)
        done.append(dim)
    return x


def cross_inner(padded):
    return padded[:, 2:, 1:-1] + padded[:, :-2, 1:-1] + padded[:, 1:-1, 2:] + padded[:, 1:-1, :-2]


def cross_local(field):
    return cross_inner(jnp.pad(field, ((0, 0), (1, 1), (1, 1))))


def chebyshev(start, residual, operate):
    center = 0.5 * (UPPER_BOUND + LOWER_BOUND)
    half_span = 0.5 * (UPPER_BOUND - LOWER_BOUND)
    sigma_ratio = center / half_span
    ratio_old = 1.0 / sigma_ratio
    update = residual / center
    result = start + update
    for sweep in range(SMOOTH - 1):
        residual = residual - operate(update)
        ratio_new = 1.0 / (2.0 * sigma_ratio - ratio_old)
        update = ratio_new * ratio_old * update + 2.0 * ratio_new / half_span * residual
        result = result + update
        ratio_old = ratio_new
    return result


def restrict(residual):
    goals, height, width = residual.shape
    blocks = residual.reshape(goals, height // COARSEN, COARSEN, width // COARSEN, COARSEN)
    return blocks.mean(axis=(2, 4))


def prolong(estimate, open_cells):
    expanded = jnp.repeat(jnp.repeat(estimate, COARSEN, axis=1), COARSEN, axis=2)
    return open_cells * expanded


def column_mask(width, reach):
    column = lax.axis_index("gy") * width + jnp.arange(width + 2 * reach, dtype=jnp.int32) - reach
    return ((column >= 0) & (column < lax.axis_size("gy") * width)).astype(jnp.float32)[
        None, None, :
    ]


def coarse_solve(coarse_rhs):
    center_weight = 4.0 + COARSE_SHIFT
    reach = CSWEEPS - 1
    width = coarse_rhs.shape[2]
    widened = with_halo(coarse_rhs, (("gy", 2),), reach)
    col_mask = column_mask(width, reach)
    extended = with_halo(widened, (("gx", 1),), reach)
    height = widened.shape[1]
    position = (
        lax.axis_index("gx") * height + jnp.arange(height + 2 * reach, dtype=jnp.int32) - reach
    )
    within = ((position >= 0) & (position < lax.axis_size("gx") * height)).astype(jnp.float32)[
        None, :, None
    ]
    within = within * col_mask
    estimate = DAMPING * extended / center_weight * within
    for sweep in range(reach):
        estimate = (
            estimate
            + DAMPING
            * (extended - (center_weight * estimate - cross_local(estimate)))
            / center_weight
        ) * within
    return estimate[:, reach : reach + height, reach : reach + width]


def per_device(obstacles, load, exit_rows, exit_cols):
    tile_rows, tile_cols = obstacles.shape
    goals = exit_rows.shape[0]
    open_int = 1 - obstacles
    margin = SMOOTH - 1
    walls = with_halo(open_int, (("gx", 0), ("gy", 1)), margin + 1).astype(jnp.float32)
    wide_rows = tile_rows + 2 * margin
    wide_cols = tile_cols + 2 * margin
    open_wide = walls[1:-1, 1:-1]
    neighbours = walls[2:, 1:-1] + walls[:-2, 1:-1] + walls[1:-1, 2:] + walls[1:-1, :-2]
    local_rows = exit_rows - lax.axis_index("gx") * tile_rows + margin
    local_cols = exit_cols - lax.axis_index("gy") * tile_cols + margin
    inside = (
        (local_rows >= 0) & (local_rows < wide_rows) & (local_cols >= 0) & (local_cols < wide_cols)
    )
    flat_index = jnp.where(inside, local_rows * wide_cols + local_cols, wide_rows * wide_cols)
    goal_index = jnp.broadcast_to(jnp.arange(goals, dtype=jnp.int32)[:, None], flat_index.shape)
    marks = (
        jnp.zeros((goals, wide_rows * wide_cols), jnp.float32)
        .at[goal_index, flat_index]
        .add(1.0, mode="drop")
    )
    exits = jnp.minimum(marks, 1.0).reshape(goals, wide_rows, wide_cols)
    diag_wide = (
        SCREENING + 4.0 * (1.0 - open_wide) + open_wide * neighbours + EXIT_SINK * open_wide * exits
    )
    open_cells = open_wide[margin : margin + tile_rows, margin : margin + tile_cols]
    diagonal = diag_wide[:, margin : margin + tile_rows, margin : margin + tile_cols]

    def operate_wide(field):
        return diag_wide * field - open_wide * cross_local(open_wide * field)

    def smooth(start, residual):
        extended = with_halo(residual, (("gx", 1), ("gy", 2)), margin)
        start_wide = jnp.pad(start, ((0, 0), (margin, margin), (margin, margin)))
        result = chebyshev(start_wide, extended, operate_wide)
        return result[:, margin : margin + tile_rows, margin : margin + tile_cols]

    source = jnp.broadcast_to(open_cells * load, (goals, tile_rows, tile_cols))
    potential = smooth(jnp.zeros_like(source), source)
    estimate = coarse_solve(restrict(source))
    correction = prolong(estimate, open_cells)
    padded_pair = (
        with_halo_2(open_cells * potential, (("gx", 1), ("gy", 2)), 1),
        with_halo_2(open_cells * correction, (("gx", 1), ("gy", 2)), 1),
    )
    residual = source - (diagonal * potential - open_cells * cross_inner(padded_pair[0]))
    shifted = residual - (diagonal * correction - open_cells * cross_inner(padded_pair[1]))
    estimate_next = coarse_solve(restrict(residual))
    potential = smooth(potential + correction, shifted)
    return potential + prolong(estimate_next, open_cells)


def solution(mesh):
    in_specs = (P("gx", "gy"), P("gx", "gy"), P(), P())
    out_specs = P(None, "gx", "gy")
    return jax.shard_map(
        per_device, mesh=mesh, in_specs=in_specs, out_specs=out_specs, check_vma=False
    )
```

profile of v0, /device:TPU:31, one launch (start us, length us, event | category | flops | bytes accessed | tf_op | source)
XLA Modules:
  0.0 296.4 jit_solution(3325423276919000334)
XLA Ops:
  0.9 5.2 %collective-permute-start = (s32[4,256]{1,0:T(4,128)S(1)}, s32[4,256]{1,0:T(4,128)S(1)}, u32[]{:S(2)}, u32[]{:S(2)}) collective-permute-start(s32[4,256]{1,0:T(4,128)S(1)} %get-tuple-element.59), channel_id=1, source_target_pairs={{0,16},{16,32},{32,48},{48,64},{64,80},{80,96},{96,112},{112,128},... | collective-permute-start | bytes 12296 | tf_op jit(solution)/shard_map/ppermute | solution.py:26
  6.2 1.9 collective-permute-start.1
  10.7 85.9 %scatter_custom_fusion = f32[140432]{0:T(1024)S(1)} fusion(s32[16384]{0:T(1024)S(1)} %bitcast.13, f32[16384]{0:T(1024)S(1)} %broadcast.247, f32[]{:T(128)} %constant.29.clone.1), kind=kCustom, calls=%fused_computation.80 | custom fusion | flops 16384 | bytes 561732
  96.9 4.0 %collective-permute-start.2 = (s32[136,4]{1,0:T(8,128)S(1)}, s32[136,4]{1,0:T(8,128)S(1)}, u32[]{:S(2)}, u32[]{:S(2)}) collective-permute-start(s32[136,4]{1,0:T(8,128)S(1)} %get-tuple-element.55), channel_id=1, source_target_pairs={{0,1},{1,2},{2,3},{3,4},{4,5},{5,6},{6,7},{7,8},{8,9},{9,10},{10,1... | collective-permute-start | bytes 6536 | tf_op jit(solution)/shard_map/ppermute | solution.py:26
  100.9 9.1 %collective-permute-start.3 = (s32[136,4]{1,0:T(8,128)S(1)}, s32[136,4]{1,0:T(8,128)S(1)}, u32[]{:S(2)}, u32[]{:S(2)}) collective-permute-start(s32[136,4]{1,0:T(8,128)S(1)} %get-tuple-element.56), channel_id=1, source_target_pairs={{1,0},{2,1},{3,2},{4,3},{5,4},{6,5},{7,6},{8,7},{9,8},{10,9},{11,1... | collective-permute-start | bytes 6536 | tf_op jit(solution)/shard_map/ppermute | solution.py:27
  113.0 5.7 %broadcast_in_dim.39 = f32[32,4,64,4]{3,2,1,0:T(8,128)} reshape(f32[128,256]{1,0:T(8,128)S(1)} %get-tuple-element.50) | data formatting | bytes 262144 | tf_op jit(solution)/shard_map/broadcast_in_dim | solution.py:158
  118.7 2.5 reduce_sum.24
  123.3 7.6 %collective-permute-start.9 = (f32[4,32,3]{2,1,0:T(8,128)S(1)}, f32[4,32,3]{2,1,0:T(8,128)S(1)}, u32[]{:S(2)}, u32[]{:S(2)}) collective-permute-start(f32[4,32,3]{2,1,0:T(8,128)S(1)} %reduce_sum.27), channel_id=1, source_target_pairs={{1,0},{2,1},{3,2},{4,3},{5,4},{6,5},{7,6},{8,7},{9,8},{10,9},{11,1... | collective-permute-start | bytes 4616 | tf_op jit(solution)/shard_map/ppermute | solution.py:27
  132.3 6.4 %collective-permute-start.10 = (f32[4,3,70]{2,1,0:T(4,128)S(1)}, f32[4,3,70]{2,1,0:T(4,128)S(1)}, u32[]{:S(2)}, u32[]{:S(2)}) collective-permute-start(f32[4,3,70]{2,1,0:T(4,128)S(1)} %get-tuple-element.53), channel_id=1, source_target_pairs={{0,16},{16,32},{32,48},{48,64},{64,80},{80,96},{96,112},{112,128},... | collective-permute-start | bytes 10088 | tf_op jit(solution)/shard_map/ppermute | solution.py:26
  138.7 1.9 collective-permute-start.11
  140.7 5.8 %collective-permute-start.4 = (f32[4,3,256]{2,1,0:T(4,128)S(1)}, f32[4,3,256]{2,1,0:T(4,128)S(1)}, u32[]{:S(2)}, u32[]{:S(2)}) collective-permute-start(f32[4,3,256]{2,1,0:T(4,128)S(1)} %broadcast_in_dim.31), channel_id=1, source_target_pairs={{0,16},{16,32},{32,48},{48,64},{64,80},{80,96},{96,112},{112,128},... | collective-permute-start | bytes 36872 | tf_op jit(solution)/shard_map/ppermute | solution.py:26
  148.9 4.7 %collective-permute-done.5 = f32[4,3,256]{2,1,0:T(4,128)S(1)} collective-permute-done((f32[4,3,256]{2,1,0:T(4,128)S(1)}, f32[4,3,256]{2,1,0:T(4,128)S(1)}, u32[]{:S(2)}, u32[]{:S(2)}) %collective-permute-start.5) | collective-permute-done | bytes 12320 | tf_op jit(solution)/shard_map/ppermute | solution.py:27
  156.5 8.2 %collective-permute-start.7 = (f32[4,134,3]{2,1,0:T(8,128)}, f32[4,134,3]{2,1,0:T(8,128)}, u32[]{:S(2)}, u32[]{:S(2)}) collective-permute-start(f32[4,134,3]{2,1,0:T(8,128)} %get-tuple-element.34), channel_id=1, source_target_pairs={{1,0},{2,1},{3,2},{4,3},{5,4},{6,5},{7,6},{8,7},{9,8},{10,9},{11,1... | collective-permute-start | bytes 19304 | tf_op jit(solution)/shard_map/ppermute | solution.py:27
  169.9 2.1 broadcast_multiply_fusion.5
  173.2 2.7 multiply_add_fusion.5
  176.1 7.4 %collective-permute-start.14 = (f32[4,128,1]{2,1,0:T(8,128)S(1)}, f32[4,128,1]{2,1,0:T(8,128)S(1)}, u32[]{:S(2)}, u32[]{:S(2)}) collective-permute-start(f32[4,128,1]{2,1,0:T(8,128)S(1)} %get-tuple-element.37), channel_id=1, source_target_pairs={{1,0},{2,1},{3,2},{4,3},{5,4},{6,5},{7,6},{8,7},{9,8},{10,9},{11,1... | collective-permute-start | bytes 6152 | tf_op jit(solution)/shard_map/ppermute | solution.py:41
  183.6 1.9 collective-permute-start.15
  185.6 1.9 collective-permute-start.12
  187.6 5.8 %collective-permute-start.13 = (f32[4,1,256]{2,1,0:T(1,128)S(1)}, f32[4,1,256]{2,1,0:T(1,128)S(1)}, u32[]{:S(2)}, u32[]{:S(2)}) collective-permute-start(f32[4,1,256]{2,1,0:T(1,128)S(1)} %get-tuple-element.39), channel_id=1, source_target_pairs={{0,16},{16,32},{32,48},{48,64},{64,80},{80,96},{96,112},{112,128},... | collective-permute-start | bytes 12296 | tf_op jit(solution)/shard_map/ppermute | solution.py:40
  193.3 7.0 %collective-permute-start.18 = (f32[4,128,1]{2,1,0:T(8,128)S(1)}, f32[4,128,1]{2,1,0:T(8,128)S(1)}, u32[]{:S(2)}, u32[]{:S(2)}) collective-permute-start(f32[4,128,1]{2,1,0:T(8,128)S(1)} %get-tuple-element.41), channel_id=1, source_target_pairs={{1,0},{2,1},{3,2},{4,3},{5,4},{6,5},{7,6},{8,7},{9,8},{10,9},{11,1... | collective-permute-start | bytes 6152 | tf_op jit(solution)/shard_map/ppermute | solution.py:41
  202.3 5.8 %collective-permute-start.17 = (f32[4,1,256]{2,1,0:T(1,128)S(1)}, f32[4,1,256]{2,1,0:T(1,128)S(1)}, u32[]{:S(2)}, u32[]{:S(2)}) collective-permute-start(f32[4,1,256]{2,1,0:T(1,128)S(1)} %get-tuple-element.43), channel_id=1, source_target_pairs={{0,16},{16,32},{32,48},{48,64},{64,80},{80,96},{96,112},{112,128},... | collective-permute-start | bytes 12296 | tf_op jit(solution)/shard_map/ppermute | solution.py:40
  208.0 2.1 collective-permute-start.19
  210.1 8.6 %collective-permute-done.19 = f32[4,128,1]{2,1,0:T(8,128)S(1)} collective-permute-done((f32[4,128,1]{2,1,0:T(8,128)S(1)}, f32[4,128,1]{2,1,0:T(8,128)S(1)}, u32[]{:S(2)}, u32[]{:S(2)}) %collective-permute-start.19) | collective-permute-done | bytes 2080 | tf_op jit(solution)/shard_map/ppermute | solution.py:40
  219.7 18.6 %reshape.89 = f32[4,32,4,64,4]{4,3,2,1,0:T(8,128)} reshape(f32[4,128,256]{2,1,0:T(8,128)S(1)} %get-tuple-element.16) | data formatting | bytes 1048576 | tf_op jit(solution)/shard_map/reshape | solution.py:78
  238.4 7.1 %reduce_sum.28 = f32[4,32,64]{2,1,0:T(8,128)S(1)} reduce(f32[4,32,4,64,4]{4,3,2,1,0:T(8,128)} %reshape.89, f32[]{:T(128)} %constant.29.clone.1), dimensions={2,4}, to_apply=%region_2.3 | reduce | flops 122880 | bytes 557060 | tf_op jit(solution)/shard_map/reduce_sum | solution.py:79
  247.5 7.0 %collective-permute-start.25 = (f32[4,32,3]{2,1,0:T(8,128)S(1)}, f32[4,32,3]{2,1,0:T(8,128)S(1)}, u32[]{:S(2)}, u32[]{:S(2)}) collective-permute-start(f32[4,32,3]{2,1,0:T(8,128)S(1)} %get-tuple-element.66), channel_id=1, source_target_pairs={{1,0},{2,1},{3,2},{4,3},{5,4},{6,5},{7,6},{8,7},{9,8},{10,9},{11,1... | collective-permute-start | bytes 4616 | tf_op jit(solution)/shard_map/ppermute | solution.py:27
  255.8 4.2 %collective-permute-start.26 = (f32[4,3,70]{2,1,0:T(4,128)S(1)}, f32[4,3,70]{2,1,0:T(4,128)S(1)}, u32[]{:S(2)}, u32[]{:S(2)}) collective-permute-start(f32[4,3,70]{2,1,0:T(4,128)S(1)} %get-tuple-element.51), channel_id=1, source_target_pairs={{0,16},{16,32},{32,48},{48,64},{64,80},{80,96},{96,112},{112,128},... | collective-permute-start | bytes 10088 | tf_op jit(solution)/shard_map/ppermute | solution.py:26
  262.0 5.8 %collective-permute-start.20 = (f32[4,3,256]{2,1,0:T(4,128)S(1)}, f32[4,3,256]{2,1,0:T(4,128)S(1)}, u32[]{:S(2)}, u32[]{:S(2)}) collective-permute-start(f32[4,3,256]{2,1,0:T(4,128)S(1)} %get-tuple-element.35), channel_id=1, source_target_pairs={{0,16},{16,32},{32,48},{48,64},{64,80},{80,96},{96,112},{112,128},... | collective-permute-start | bytes 36872 | tf_op jit(solution)/shard_map/ppermute | solution.py:26
  267.8 1.9 collective-permute-start.21
  270.2 4.7 %collective-permute-done.21 = f32[4,3,256]{2,1,0:T(4,128)S(1)} collective-permute-done((f32[4,3,256]{2,1,0:T(4,128)S(1)}, f32[4,3,256]{2,1,0:T(4,128)S(1)}, u32[]{:S(2)}, u32[]{:S(2)}) %collective-permute-start.21) | collective-permute-done | bytes 12320 | tf_op jit(solution)/shard_map/ppermute | solution.py:27
  277.8 8.2 %collective-permute-start.23 = (f32[4,134,3]{2,1,0:T(8,128)}, f32[4,134,3]{2,1,0:T(8,128)}, u32[]{:S(2)}, u32[]{:S(2)}) collective-permute-start(f32[4,134,3]{2,1,0:T(8,128)} %get-tuple-element.32), channel_id=1, source_target_pairs={{1,0},{2,1},{3,2},{4,3},{5,4},{6,5},{7,6},{8,7},{9,8},{10,9},{11,1... | collective-permute-start | bytes 19304 | tf_op jit(solution)/shard_map/ppermute | solution.py:27
  291.3 1.9 broadcast_multiply_fusion.2
  (111 shorter events, 41.9 us)
Async XLA Ops:
  0.9 95.9 %collective-permute-start = (s32[4,256]{1,0:T(4,128)S(1)}, s32[4,256]{1,0:T(4,128)S(1)}, u32[]{:S(2)}, u32[]{:S(2)}) collective-permute-start(s32[4,256]{1,0:T(4,128)S(1)} %get-tuple-element.59), channel_id=1, source_target_pairs={{0,16},{16,32},{32,48},{48,64},{64,80},{80,96},{96,112},{112,128},... | collective-permute-start | bytes 12296 | tf_op jit(solution)/shard_map/ppermute | solution.py:26
  6.2 90.6 %collective-permute-start.1 = (s32[4,256]{1,0:T(4,128)S(1)}, s32[4,256]{1,0:T(4,128)S(1)}, u32[]{:S(2)}, u32[]{:S(2)}) collective-permute-start(s32[4,256]{1,0:T(4,128)S(1)} %get-tuple-element.60), channel_id=1, source_target_pairs={{16,0},{32,16},{48,32},{64,48},{80,64},{96,80},{112,96},{128,112},... | collective-permute-start | bytes 12296 | tf_op jit(solution)/shard_map/ppermute | solution.py:27
  96.9 14.6 %collective-permute-start.2 = (s32[136,4]{1,0:T(8,128)S(1)}, s32[136,4]{1,0:T(8,128)S(1)}, u32[]{:S(2)}, u32[]{:S(2)}) collective-permute-start(s32[136,4]{1,0:T(8,128)S(1)} %get-tuple-element.55), channel_id=1, source_target_pairs={{0,1},{1,2},{2,3},{3,4},{4,5},{5,6},{6,7},{7,8},{8,9},{9,10},{10,1... | collective-permute-start | bytes 6536 | tf_op jit(solution)/shard_map/ppermute | solution.py:26
  100.9 11.0 %collective-permute-start.3 = (s32[136,4]{1,0:T(8,128)S(1)}, s32[136,4]{1,0:T(8,128)S(1)}, u32[]{:S(2)}, u32[]{:S(2)}) collective-permute-start(s32[136,4]{1,0:T(8,128)S(1)} %get-tuple-element.56), channel_id=1, source_target_pairs={{1,0},{2,1},{3,2},{4,3},{5,4},{6,5},{7,6},{8,7},{9,8},{10,9},{11,1... | collective-permute-start | bytes 6536 | tf_op jit(solution)/shard_map/ppermute | solution.py:27
  111.5 58.4 %copy-start.2 = (f32[32,64]{1,0:T(8,128)}, f32[32,64]{1,0:T(8,128)S(1)}, u32[]{:S(2)}) copy-start(f32[32,64]{1,0:T(8,128)S(1)} %slice.421) | copy-start | bytes 24580
  121.4 10.6 %collective-permute-start.8 = (f32[4,32,3]{2,1,0:T(8,128)S(1)}, f32[4,32,3]{2,1,0:T(8,128)S(1)}, u32[]{:S(2)}, u32[]{:S(2)}) collective-permute-start(f32[4,32,3]{2,1,0:T(8,128)S(1)} %reduce_sum.25), channel_id=1, source_target_pairs={{0,1},{1,2},{2,3},{3,4},{4,5},{5,6},{6,7},{7,8},{8,9},{9,10},{10,1... | collective-permute-start | bytes 4616 | tf_op jit(solution)/shard_map/ppermute | solution.py:26
  123.3 8.9 %collective-permute-start.9 = (f32[4,32,3]{2,1,0:T(8,128)S(1)}, f32[4,32,3]{2,1,0:T(8,128)S(1)}, u32[]{:S(2)}, u32[]{:S(2)}) collective-permute-start(f32[4,32,3]{2,1,0:T(8,128)S(1)} %reduce_sum.27), channel_id=1, source_target_pairs={{1,0},{2,1},{3,2},{4,3},{5,4},{6,5},{7,6},{8,7},{9,8},{10,9},{11,1... | collective-permute-start | bytes 4616 | tf_op jit(solution)/shard_map/ppermute | solution.py:27
  131.9 38.0 %copy-start.1 = (f32[134,262]{1,0:T(8,128)}, f32[134,262]{1,0:T(8,128)S(1)}, u32[]{:S(2)}) copy-start(f32[134,262]{1,0:T(8,128)S(1)} %get-tuple-element.47) | copy-start | bytes 421300
  132.3 16.1 %collective-permute-start.10 = (f32[4,3,70]{2,1,0:T(4,128)S(1)}, f32[4,3,70]{2,1,0:T(4,128)S(1)}, u32[]{:S(2)}, u32[]{:S(2)}) collective-permute-start(f32[4,3,70]{2,1,0:T(4,128)S(1)} %get-tuple-element.53), channel_id=1, source_target_pairs={{0,16},{16,32},{32,48},{48,64},{64,80},{80,96},{96,112},{112,128},... | collective-permute-start | bytes 10088 | tf_op jit(solution)/shard_map/ppermute | solution.py:26
  138.7 9.7 %collective-permute-start.11 = (f32[4,3,70]{2,1,0:T(4,128)S(1)}, f32[4,3,70]{2,1,0:T(4,128)S(1)}, u32[]{:S(2)}, u32[]{:S(2)}) collective-permute-start(f32[4,3,70]{2,1,0:T(4,128)S(1)} %get-tuple-element.54), channel_id=1, source_target_pairs={{16,0},{32,16},{48,32},{64,48},{80,64},{96,80},{112,96},{128,112},... | collective-permute-start | bytes 10088 | tf_op jit(solution)/shard_map/ppermute | solution.py:27
  140.7 8.2 %collective-permute-start.4 = (f32[4,3,256]{2,1,0:T(4,128)S(1)}, f32[4,3,256]{2,1,0:T(4,128)S(1)}, u32[]{:S(2)}, u32[]{:S(2)}) collective-permute-start(f32[4,3,256]{2,1,0:T(4,128)S(1)} %broadcast_in_dim.31), channel_id=1, source_target_pairs={{0,16},{16,32},{32,48},{48,64},{64,80},{80,96},{96,112},{112,128},... | collective-permute-start | bytes 36872 | tf_op jit(solution)/shard_map/ppermute | solution.py:26
  146.4 7.2 %collective-permute-start.5 = (f32[4,3,256]{2,1,0:T(4,128)S(1)}, f32[4,3,256]{2,1,0:T(4,128)S(1)}, u32[]{:S(2)}, u32[]{:S(2)}) collective-permute-start(f32[4,3,256]{2,1,0:T(4,128)S(1)} %broadcast_in_dim.33), channel_id=1, source_target_pairs={{16,0},{32,16},{48,32},{64,48},{80,64},{96,80},{112,96},{128,112},... | collective-permute-start | bytes 36872 | tf_op jit(solution)/shard_map/ppermute | solution.py:27
  154.6 12.3 %collective-permute-start.6 = (f32[4,134,3]{2,1,0:T(8,128)}, f32[4,134,3]{2,1,0:T(8,128)S(1)}, u32[]{:S(2)}, u32[]{:S(2)}) collective-permute-start(f32[4,134,3]{2,1,0:T(8,128)} %get-tuple-element.33), channel_id=1, source_target_pairs={{0,1},{1,2},{2,3},{3,4},{4,5},{5,6},{6,7},{7,8},{8,9},{9,10},{10,1... | collective-permute-start | bytes 19304 | tf_op jit(solution)/shard_map/ppermute | solution.py:26
  156.5 12.0 %collective-permute-start.7 = (f32[4,134,3]{2,1,0:T(8,128)}, f32[4,134,3]{2,1,0:T(8,128)}, u32[]{:S(2)}, u32[]{:S(2)}) collective-permute-start(f32[4,134,3]{2,1,0:T(8,128)} %get-tuple-element.34), channel_id=1, source_target_pairs={{1,0},{2,1},{3,2},{4,3},{5,4},{6,5},{7,6},{8,7},{9,8},{10,9},{11,1... | collective-permute-start | bytes 19304 | tf_op jit(solution)/shard_map/ppermute | solution.py:27
  176.1 24.2 %collective-permute-start.14 = (f32[4,128,1]{2,1,0:T(8,128)S(1)}, f32[4,128,1]{2,1,0:T(8,128)S(1)}, u32[]{:S(2)}, u32[]{:S(2)}) collective-permute-start(f32[4,128,1]{2,1,0:T(8,128)S(1)} %get-tuple-element.37), channel_id=1, source_target_pairs={{1,0},{2,1},{3,2},{4,3},{5,4},{6,5},{7,6},{8,7},{9,8},{10,9},{11,1... | collective-permute-start | bytes 6152 | tf_op jit(solution)/shard_map/ppermute | solution.py:41
  183.6 18.7 %collective-permute-start.15 = (f32[4,128,1]{2,1,0:T(8,128)S(1)}, f32[4,128,1]{2,1,0:T(8,128)S(1)}, u32[]{:S(2)}, u32[]{:S(2)}) collective-permute-start(f32[4,128,1]{2,1,0:T(8,128)S(1)} %get-tuple-element.38), channel_id=1, source_target_pairs={{0,1},{1,2},{2,3},{3,4},{4,5},{5,6},{6,7},{7,8},{8,9},{9,10},{10,1... | collective-permute-start | bytes 6152 | tf_op jit(solution)/shard_map/ppermute | solution.py:40
  185.6 33.1 %collective-permute-start.12 = (f32[4,1,256]{2,1,0:T(1,128)S(1)}, f32[4,1,256]{2,1,0:T(1,128)S(1)}, u32[]{:S(2)}, u32[]{:S(2)}) collective-permute-start(f32[4,1,256]{2,1,0:T(1,128)S(1)} %get-tuple-element.40), channel_id=1, source_target_pairs={{16,0},{32,16},{48,32},{64,48},{80,64},{96,80},{112,96},{128,112},... | collective-permute-start | bytes 12296 | tf_op jit(solution)/shard_map/ppermute | solution.py:41
  187.6 31.2 %collective-permute-start.13 = (f32[4,1,256]{2,1,0:T(1,128)S(1)}, f32[4,1,256]{2,1,0:T(1,128)S(1)}, u32[]{:S(2)}, u32[]{:S(2)}) collective-permute-start(f32[4,1,256]{2,1,0:T(1,128)S(1)} %get-tuple-element.39), channel_id=1, source_target_pairs={{0,16},{16,32},{32,48},{48,64},{64,80},{80,96},{96,112},{112,128},... | collective-permute-start | bytes 12296 | tf_op jit(solution)/shard_map/ppermute | solution.py:40
  193.3 14.7 %collective-permute-start.18 = (f32[4,128,1]{2,1,0:T(8,128)S(1)}, f32[4,128,1]{2,1,0:T(8,128)S(1)}, u32[]{:S(2)}, u32[]{:S(2)}) collective-permute-start(f32[4,128,1]{2,1,0:T(8,128)S(1)} %get-tuple-element.41), channel_id=1, source_target_pairs={{1,0},{2,1},{3,2},{4,3},{5,4},{6,5},{7,6},{8,7},{9,8},{10,9},{11,1... | collective-permute-start | bytes 6152 | tf_op jit(solution)/shard_map/ppermute | solution.py:41
  200.3 18.4 %collective-permute-start.16 = (f32[4,1,256]{2,1,0:T(1,128)S(1)}, f32[4,1,256]{2,1,0:T(1,128)S(1)}, u32[]{:S(2)}, u32[]{:S(2)}) collective-permute-start(f32[4,1,256]{2,1,0:T(1,128)S(1)} %get-tuple-element.44), channel_id=1, source_target_pairs={{16,0},{32,16},{48,32},{64,48},{80,64},{96,80},{112,96},{128,112},... | collective-permute-start | bytes 12296 | tf_op jit(solution)/shard_map/ppermute | solution.py:41
  202.3 16.5 %collective-permute-start.17 = (f32[4,1,256]{2,1,0:T(1,128)S(1)}, f32[4,1,256]{2,1,0:T(1,128)S(1)}, u32[]{:S(2)}, u32[]{:S(2)}) collective-permute-start(f32[4,1,256]{2,1,0:T(1,128)S(1)} %get-tuple-element.43), channel_id=1, source_target_pairs={{0,16},{16,32},{32,48},{48,64},{64,80},{80,96},{96,112},{112,128},... | collective-permute-start | bytes 12296 | tf_op jit(solution)/shard_map/ppermute | solution.py:40
  208.0 10.7 %collective-permute-start.19 = (f32[4,128,1]{2,1,0:T(8,128)S(1)}, f32[4,128,1]{2,1,0:T(8,128)S(1)}, u32[]{:S(2)}, u32[]{:S(2)}) collective-permute-start(f32[4,128,1]{2,1,0:T(8,128)S(1)} %get-tuple-element.42), channel_id=1, source_target_pairs={{0,1},{1,2},{2,3},{3,4},{4,5},{5,6},{6,7},{7,8},{8,9},{9,10},{10,1... | collective-permute-start | bytes 6152 | tf_op jit(solution)/shard_map/ppermute | solution.py:40
  219.7 66.3 %copy-start.3 = (f32[32,64]{1,0:T(8,128)S(1)}, f32[32,64]{1,0:T(8,128)}, u32[]{:S(2)}) copy-start(f32[32,64]{1,0:T(8,128)} %copy-done.2) | copy-start | bytes 24580
  238.4 56.1 %copy-start = (f32[4,128,256]{2,1,0:T(8,128)S(1)}, f32[4,128,256]{2,1,0:T(8,128)}, u32[]{:S(2)}) copy-start(f32[4,128,256]{2,1,0:T(8,128)} %get-tuple-element.10) | copy-start | bytes 1572868
  245.5 8.9 %collective-permute-start.24 = (f32[4,32,3]{2,1,0:T(8,128)S(1)}, f32[4,32,3]{2,1,0:T(8,128)S(1)}, u32[]{:S(2)}, u32[]{:S(2)}) collective-permute-start(f32[4,32,3]{2,1,0:T(8,128)S(1)} %get-tuple-element.65), channel_id=1, source_target_pairs={{0,1},{1,2},{2,3},{3,4},{4,5},{5,6},{6,7},{7,8},{8,9},{9,10},{10,1... | collective-permute-start | bytes 4616 | tf_op jit(solution)/shard_map/ppermute | solution.py:26
  247.5 8.3 %collective-permute-start.25 = (f32[4,32,3]{2,1,0:T(8,128)S(1)}, f32[4,32,3]{2,1,0:T(8,128)S(1)}, u32[]{:S(2)}, u32[]{:S(2)}) collective-permute-start(f32[4,32,3]{2,1,0:T(8,128)S(1)} %get-tuple-element.66), channel_id=1, source_target_pairs={{1,0},{2,1},{3,2},{4,3},{5,4},{6,5},{7,6},{8,7},{9,8},{10,9},{11,1... | collective-permute-start | bytes 4616 | tf_op jit(solution)/shard_map/ppermute | solution.py:27
  255.8 13.8 %collective-permute-start.26 = (f32[4,3,70]{2,1,0:T(4,128)S(1)}, f32[4,3,70]{2,1,0:T(4,128)S(1)}, u32[]{:S(2)}, u32[]{:S(2)}) collective-permute-start(f32[4,3,70]{2,1,0:T(4,128)S(1)} %get-tuple-element.51), channel_id=1, source_target_pairs={{0,16},{16,32},{32,48},{48,64},{64,80},{80,96},{96,112},{112,128},... | collective-permute-start | bytes 10088 | tf_op jit(solution)/shard_map/ppermute | solution.py:26
  260.1 9.6 %collective-permute-start.27 = (f32[4,3,70]{2,1,0:T(4,128)S(1)}, f32[4,3,70]{2,1,0:T(4,128)S(1)}, u32[]{:S(2)}, u32[]{:S(2)}) collective-permute-start(f32[4,3,70]{2,1,0:T(4,128)S(1)} %get-tuple-element.52), channel_id=1, source_target_pairs={{16,0},{32,16},{48,32},{64,48},{80,64},{96,80},{112,96},{128,112},... | collective-permute-start | bytes 10088 | tf_op jit(solution)/shard_map/ppermute | solution.py:27
  262.0 8.2 %collective-permute-start.20 = (f32[4,3,256]{2,1,0:T(4,128)S(1)}, f32[4,3,256]{2,1,0:T(4,128)S(1)}, u32[]{:S(2)}, u32[]{:S(2)}) collective-permute-start(f32[4,3,256]{2,1,0:T(4,128)S(1)} %get-tuple-element.35), channel_id=1, source_target_pairs={{0,16},{16,32},{32,48},{48,64},{64,80},{80,96},{96,112},{112,128},... | collective-permute-start | bytes 36872 | tf_op jit(solution)/shard_map/ppermute | solution.py:26
  267.8 7.2 %collective-permute-start.21 = (f32[4,3,256]{2,1,0:T(4,128)S(1)}, f32[4,3,256]{2,1,0:T(4,128)S(1)}, u32[]{:S(2)}, u32[]{:S(2)}) collective-permute-start(f32[4,3,256]{2,1,0:T(4,128)S(1)} %get-tuple-element.36), channel_id=1, source_target_pairs={{16,0},{32,16},{48,32},{64,48},{80,64},{96,80},{112,96},{128,112},... | collective-permute-start | bytes 36872 | tf_op jit(solution)/shard_map/ppermute | solution.py:27
  275.9 12.4 %collective-permute-start.22 = (f32[4,134,3]{2,1,0:T(8,128)}, f32[4,134,3]{2,1,0:T(8,128)}, u32[]{:S(2)}, u32[]{:S(2)}) collective-permute-start(f32[4,134,3]{2,1,0:T(8,128)} %get-tuple-element.31), channel_id=1, source_target_pairs={{0,1},{1,2},{2,3},{3,4},{4,5},{5,6},{6,7},{7,8},{8,9},{9,10},{10,1... | collective-permute-start | bytes 19304 | tf_op jit(solution)/shard_map/ppermute | solution.py:26
  277.8 12.0 %collective-permute-start.23 = (f32[4,134,3]{2,1,0:T(8,128)}, f32[4,134,3]{2,1,0:T(8,128)}, u32[]{:S(2)}, u32[]{:S(2)}) collective-permute-start(f32[4,134,3]{2,1,0:T(8,128)} %get-tuple-element.32), channel_id=1, source_target_pairs={{1,0},{2,1},{3,2},{4,3},{5,4},{6,5},{7,6},{8,7},{9,8},{10,9},{11,1... | collective-permute-start | bytes 19304 | tf_op jit(solution)/shard_map/ppermute | solution.py:27
where the time goes:
time: 297 us; the launch traced here: 296 us
  starting transfers between devices  122 us (41%)
  other arithmetic  118 us (40%)
  local copies, waits for them, and re-layouts  29 us (10%)
  waiting for transfers between devices  26.4 us (9%)
    unnamed x4, other arithmetic  87.5 us
    ppermute x10, starting transfers between devices, with_halo(): after = lax.ppermute(initial, axis, down)  49.7 us
    ppermute x10, starting transfers between devices, with_halo(): before = lax.ppermute(last, axis, up)  39 us
    reshape x1, local copies, waits for them, and re-layouts, restrict(): residual.reshape(goals, height // COARSEN, COARSEN, width // COARSEN, COA...  18.6 us
    ppermute x4, starting transfers between devices, with_halo_2(): lax.ppermute(initial, axis, [(b, a) for a, b in up])  18.2 us
    ppermute x4, starting transfers between devices, with_halo_2(): lax.ppermute(last, axis, up)  15.5 us
    ppermute x10, waiting for transfers between devices, with_halo(): after = lax.ppermute(initial, axis, down)  14.5 us
    reduce_sum x2, other arithmetic, restrict(): return blocks.mean(axis=(2, 4))  9.61 us
  transfers between devices with their start and end apart: 28, of which 10 were waited for; matrix products, arithmetic and copies ran while one was open for 31% of the time, Pallas kernels for 0%

commit v1 on v0

v1 whole, which is shorter than its diff:
```python
import functools

import jax
import jax.numpy as jnp
import numpy as np
from jax import lax
from jax.experimental import pallas as pl
from jax.experimental.pallas import tpu as pltpu
from jax.sharding import PartitionSpec as P

SCREENING = 0.0001
EXIT_SINK = 4.0
WEIGHT = 4.01
DAMPING = 0.8
CENTER = 6.75
HALF = 5.75

GOALS = 4
ROWS = 128
COLS = 256
HALO = 16
WIDE = ROWS + 2 * HALO
LANES = 384
PAD = 8
CROWS = WIDE // 4
CHUNK = 16
F32 = jnp.float32
BF16 = jnp.bfloat16

COEF = []
_q = CENTER / HALF
_p = 1.0 / _q
for _ in range(3):
    _n = 1.0 / (2.0 * _q - _p)
    COEF.append((_n * _p, 2.0 * _n / HALF))
    _p = _n


def split(x):
    high = x.astype(BF16)
    return high, (x - high.astype(F32)).astype(BF16)


def dot(a, b, dims=((1,), (0,))):
    return lax.dot_general(a, b, (dims, ((), ())), preferred_element_type=F32)


def iota(shape, dim):
    return lax.broadcasted_iota(jnp.int32, shape, dim)


def one_zero(condition):
    return jnp.where(condition, 1.0, 0.0).astype(F32)


def exits_kernel(rows_ref, cols_ref, out_ref):
    row0 = lax.axis_index("gx") * ROWS - HALO
    col0 = lax.axis_index("gy") * COLS
    step = 1024
    count = rows_ref.shape[1] // step
    row_at = iota((WIDE, step), 0)
    col_at = iota((COLS + 2 * HALO, step), 0)
    lane = iota((WIDE, 128), 1)

    def goal(g, carry):
        def part(k, total):
            at = pl.ds(pl.multiple_of(k * step, step), step)
            r = rows_ref[pl.ds(g, 1), at] - row0
            c = cols_ref[pl.ds(g, 1), at] - col0
            near = (c >= -HALO) & (c < COLS + HALO)
            c = jnp.where(c < 0, c + COLS + HALO, jnp.where(c >= COLS, c + HALO, c))
            c = jnp.where(near, c, -1)
            left = one_zero(row_at == r).astype(BF16)
            right = one_zero(col_at == c).astype(BF16)
            return total + dot(left, right, ((1,), (1,)))

        total = lax.fori_loop(0, count, part, jnp.zeros((WIDE, COLS + 2 * HALO), F32))
        sink = jnp.minimum(total, 1.0) * EXIT_SINK
        out_ref[g, :, 0:COLS] = sink[:, :COLS]
        tail = jnp.concatenate([sink[:, COLS:], jnp.zeros((WIDE, 128 - 2 * HALO), F32)], axis=1)
        out_ref[g, :, COLS:LANES] = pltpu.roll(tail, 128 - HALO, 1)
        return carry

    lax.fori_loop(0, GOALS, goal, 0)


def exits_of(rows, cols):
    return pl.pallas_call(
        exits_kernel,
        out_shape=jax.ShapeDtypeStruct((GOALS, WIDE, LANES), F32),
        in_specs=[pl.BlockSpec(memory_space=pltpu.VMEM)] * 2,
        out_specs=pl.BlockSpec(memory_space=pltpu.VMEM),
        compiler_params=pltpu.CompilerParams(vmem_limit_bytes=32 * 2**20),
        cost_estimate=pl.CostEstimate(flops=2 * 4 * 4096 * 160 * 288, bytes_accessed=2**20, transcendentals=0),
    )(rows, cols)


def pack_kernel(src_ref, top_ref, bottom_ref, left_ref, right_ref):
    def tile(q, lo):
        if q < HALO // 8:
            return top_ref[8 * q : 8 * q + 8, lo : lo + 128]
        if q >= (HALO + ROWS) // 8:
            at = 8 * q - HALO - ROWS
            return bottom_ref[at : at + 8, lo : lo + 128]
        at = 8 * q - HALO
        return src_ref[at : at + 8, lo : lo + 128]

    lane = iota((8, 128), 1)
    for b in range(LANES // 128):
        left = jnp.zeros((8, 128), F32)
        right = jnp.zeros((8, 128), F32)
        for m in range(8):
            q = 8 * b + m
            if q >= WIDE // 8:
                break
            here = (lane >= HALO * m) & (lane < HALO * (m + 1))
            left = jnp.where(here, pltpu.roll(tile(q, 0), HALO * m, 1), left)
            right = jnp.where(here, pltpu.roll(tile(q, COLS - 128), (HALO * m + HALO) % 128, 1), right)
        left_ref[:, 128 * b : 128 * b + 128] = left
        right_ref[:, 128 * b : 128 * b + 128] = right


def pack(src, top, bottom):
    return pl.pallas_call(
        pack_kernel,
        out_shape=[jax.ShapeDtypeStruct((8, LANES), F32)] * 2,
        in_specs=[pl.BlockSpec(memory_space=pltpu.VMEM)] * 3,
        out_specs=[pl.BlockSpec(memory_space=pltpu.VMEM)] * 2,
    )(src, top, bottom)


def main_kernel(
    src_ref, top_ref, bottom_ref, from_left_ref, from_right_ref, exits_ref, out_ref,
    s_ref, o_ref, diag_ref, r1_ref, corr_ref, shift_ref, da_ref, db_ref, r_ref, x_ref, pool_ref, grow_ref,
):
    gx, gy = lax.axis_index("gx"), lax.axis_index("gy")
    zero = jnp.zeros((PAD, LANES), F32)
    for ref in (s_ref, o_ref, corr_ref, da_ref, db_ref):
        ref[0:PAD, :] = zero
        ref[PAD + WIDE : 2 * PAD + WIDE, :] = zero

    s_ref[PAD : PAD + HALO, 0:COLS] = top_ref[...]
    s_ref[PAD + HALO : PAD + HALO + ROWS, 0:COLS] = src_ref[...]
    s_ref[PAD + HALO + ROWS : PAD + WIDE, 0:COLS] = bottom_ref[...]
    lane = iota((8, 128), 1)
    for q in range(WIDE // 8):
        b, m = divmod(q, 8)
        at = slice(128 * b, 128 * b + 128)
        ahead = pltpu.roll(from_right_ref[:, at], (128 - HALO * m) % 128, 1)
        behind = pltpu.roll(from_left_ref[:, at], (128 - HALO - HALO * m) % 128, 1)
        both = jnp.where(lane < HALO, ahead, jnp.where(lane >= 128 - HALO, behind, 0.0))
        s_ref[PAD + 8 * q : PAD + 8 * q + 8, COLS:LANES] = both

    chunks = range(0, WIDE, CHUNK)

    def pad_at(i, shift=0):
        return slice(PAD + i + shift, PAD + i + shift + CHUNK)

    def at(i):
        return slice(i, i + CHUNK)

    def cross(ref, i, mid):
        ends = ref[pad_at(i, 1), :] + ref[pad_at(i, -1), :]
        return ends + (pltpu.roll(mid, LANES - 1, 1) + pltpu.roll(mid, 1, 1))

    for i in chunks:
        o_ref[pad_at(i), :] = one_zero(s_ref[pad_at(i), :] > 0.0)
    for i in chunks:
        o, s = o_ref[pad_at(i), :], s_ref[pad_at(i), :]
        diag = SCREENING + 4.0 * (1.0 - o) + o * cross(o_ref, i, o)
        diag_ref[at(i), :] = diag
        d = s * (1.0 / CENTER)
        r1_ref[at(i), :] = s - diag * d + o * (cross(s_ref, i, s) * (1.0 / CENTER))

    fine_col, coarse_col = iota((LANES, 128), 0), iota((LANES, 128), 1)
    fine_col = jnp.where(fine_col >= 320, fine_col - LANES, fine_col)
    coarse_col = jnp.where(coarse_col >= 96, coarse_col - 128, coarse_col)
    gather_cols = jnp.where((fine_col >> 2) == coarse_col, 0.25, 0.0).astype(BF16)
    fine_row, coarse_row = iota((CROWS, WIDE), 1), iota((CROWS, WIDE), 0)
    gather_rows = jnp.where((fine_row >> 2) == coarse_row, 0.25, 0.0).astype(BF16)
    gather_rows = jnp.concatenate([gather_rows, gather_rows], axis=1)
    spread_c, spread_f = iota((256, LANES), 0) & 127, iota((256, LANES), 1)
    spread_c = jnp.where(spread_c >= 96, spread_c - 128, spread_c)
    spread_f = jnp.where(spread_f >= 320, spread_f - LANES, spread_f)
    spread_cols = one_zero(spread_c == (spread_f >> 2)).astype(BF16)
    sr_f, sr_c = iota((WIDE, 2 * CROWS), 0), iota((WIDE, 2 * CROWS), 1)
    sr_c = jnp.where(sr_c >= CROWS, sr_c - CROWS, sr_c)
    spread_rows = one_zero((sr_f >> 2) == sr_c).astype(BF16)

    def restrict(field):
        high, low = split(field)
        part = dot(high, gather_cols) + dot(low, gather_cols)
        high, low = split(part)
        return dot(gather_rows, jnp.concatenate([high, low], axis=0))

    def prolong_cols(e):
        high, low = split(e)
        return dot(jnp.concatenate([high, low], axis=1), spread_cols)

    def prolong_rows(e, spread):
        high, low = split(e)
        return dot(spread, jnp.concatenate([high, low], axis=0))

    def coarse(f):
        n = f.shape[0]
        row = gx * (ROWS // 4) + (lax.rem(iota((n, 128), 0), CROWS) - HALO // 4)
        col = iota((n, 128), 1)
        col = gy * (COLS // 4) + jnp.where(col >= 96, col - 128, col)
        inside = (row >= 0) & (row < 32 * (ROWS // 4)) & (col >= 0) & (col < 16 * (COLS // 4))
        mask = one_zero(inside)
        f = f * (DAMPING / WEIGHT)
        e = f * mask
        for _ in range(3):
            cr = (pltpu.roll(e, n - 1, 0) + pltpu.roll(e, 1, 0)) + (pltpu.roll(e, 127, 1) + pltpu.roll(e, 1, 1))
            e = ((1.0 - DAMPING) * e + f + (DAMPING / WEIGHT) * cr) * mask
        return e

    estimate = coarse(restrict(s_ref[PAD : PAD + WIDE, :]))
    corr_ref[PAD : PAD + WIDE, :] = prolong_rows(prolong_cols(estimate), spread_rows) * o_ref[PAD : PAD + WIDE, :]
    for i in chunks:
        c = corr_ref[pad_at(i), :]
        shift_ref[at(i), :] = o_ref[pad_at(i), :] * cross(corr_ref, i, c) - diag_ref[at(i), :] * c

    def goal(g, carry):
        sink = exits_ref.at[g]

        def next_d(old_ref, new_ref, i, a, b):
            mid, o = old_ref[pad_at(i), :], o_ref[pad_at(i), :]
            diag = diag_ref[at(i), :] + o * sink[at(i), :]
            r = r_ref[at(i), :] - diag * mid + o * cross(old_ref, i, mid)
            d = a * mid + b * r
            r_ref[at(i), :] = r
            new_ref[pad_at(i), :] = d
            x_ref[g, at(i), :] += d

        (a1, b1), (a2, b2), (a3, b3) = COEF
        for i in chunks:
            s, o = s_ref[pad_at(i), :], o_ref[pad_at(i), :]
            d = s * (1.0 / CENTER)
            r = r1_ref[at(i), :] - (o * sink[at(i), :]) * d
            n = a1 * d + b1 * r
            r_ref[at(i), :] = r
            da_ref[pad_at(i), :] = n
            x_ref[g, at(i), :] = d + n
        for i in chunks:
            next_d(da_ref, db_ref, i, a2, b2)
        for i in chunks:
            next_d(db_ref, da_ref, i, a3, b3)
        for i in chunks:
            mid, o = da_ref[pad_at(i), :], o_ref[pad_at(i), :]
            hit = o * sink[at(i), :]
            r = r_ref[at(i), :] - (diag_ref[at(i), :] + hit) * mid + o * cross(da_ref, i, mid)
            pool_ref[at(i), :] = r
            c = corr_ref[pad_at(i), :]
            r = r + shift_ref[at(i), :] - hit * c
            d = r * (1.0 / CENTER)
            r_ref[at(i), :] = r
            db_ref[pad_at(i), :] = d
            x_ref[g, at(i), :] += c + d
        grow_ref[g] = restrict(pool_ref[...])
        for i in chunks:
            next_d(db_ref, da_ref, i, a1, b1)
        for i in chunks:
            next_d(da_ref, db_ref, i, a2, b2)
        for i in range(HALO, HALO + ROWS, CHUNK):
            mid, o = db_ref[pad_at(i), :], o_ref[pad_at(i), :]
            diag = diag_ref[at(i), :] + o * sink[at(i), :]
            r = r_ref[at(i), :] - diag * mid + o * cross(db_ref, i, mid)
            x_ref[g, at(i), :] += a3 * mid + b3 * r
        return carry

    lax.fori_loop(0, GOALS, goal, 0)

    after = coarse(grow_ref[...].reshape(GOALS * CROWS, 128))
    wide = prolong_cols(after)
    o = o_ref[PAD + HALO : PAD + HALO + ROWS, 0:COLS]
    for g in range(GOALS):
        add = prolong_rows(wide[g * CROWS : (g + 1) * CROWS, 0:COLS], spread_rows[HALO : HALO + ROWS])
        out_ref[g] = x_ref[g, HALO : HALO + ROWS, 0:COLS] + o * add


def main(src, top, bottom, from_left, from_right, exits):
    padded = pltpu.VMEM((WIDE + 2 * PAD, LANES), F32)
    plain = pltpu.VMEM((WIDE, LANES), F32)
    return pl.pallas_call(
        main_kernel,
        out_shape=jax.ShapeDtypeStruct((GOALS, ROWS, COLS), F32),
        in_specs=[pl.BlockSpec(memory_space=pltpu.VMEM)] * 6,
        out_specs=pl.BlockSpec(memory_space=pltpu.VMEM),
        scratch_shapes=[
            padded, padded, plain, plain, padded, plain, padded, padded, plain,
            pltpu.VMEM((GOALS, WIDE, LANES), F32), plain, pltpu.VMEM((GOALS, CROWS, 128), F32),
        ],
        compiler_params=pltpu.CompilerParams(vmem_limit_bytes=32 * 2**20),
        cost_estimate=pl.CostEstimate(flops=10**8, bytes_accessed=2**20, transcendentals=0),
    )(src, top, bottom, from_left, from_right, exits)


def per_device(obstacles, load, exit_rows, exit_cols):
    gx, gy = lax.axis_index("gx"), lax.axis_index("gy")
    ny = lax.axis_size("gy")
    source = jnp.where(obstacles == 0, load, 0.0)
    first, last = source[:HALO], source[ROWS - HALO :]
    even = lax.rem(gx, 2) == 0
    nx = lax.axis_size("gx")
    inner = [(i, i ^ 1) for i in range(nx)]
    outer = [(i, j) for i in range(1, nx - 1) for j in [((i + 1) ^ 1) - 1]]
    got_outer = lax.ppermute(jnp.where(even, first, last), "gx", outer)
    got_inner = lax.ppermute(jnp.where(even, last, first), "gx", inner)
    exits = exits_of(exit_rows, exit_cols)
    top = jnp.where(even, got_outer, got_inner)
    bottom = jnp.where(even, got_inner, got_outer)
    left, right = pack(source, top, bottom)
    from_left = lax.ppermute(right, "gy", [(i, i + 1) for i in range(ny - 1)])
    from_right = lax.ppermute(left, "gy", [(i + 1, i) for i in range(ny - 1)])
    return main(source, top, bottom, from_left, from_right, exits)


def solution(mesh):
    in_specs = (P("gx", "gy"), P("gx", "gy"), P(), P())
    out_specs = P(None, "gx", "gy")
    return jax.shard_map(
        per_device, mesh=mesh, in_specs=in_specs, out_specs=out_specs, check_vma=False
    )
```

time: 297 us -> 42.8 us (0.14)
  other arithmetic: 118 us -> 1.61 us
  starting transfers between devices: 122 us -> 20.7 us
  local copies, waits for them, and re-layouts: 29 us -> 0.03 us
  waiting for transfers between devices: 26.4 us -> 2.58 us
  Pallas kernels: 0 us -> 17.5 us
    ppermute x28 -> x4, starting transfers between devices: 122 us -> 20.7 us  [the longest x1 9.56 us: per_device(): from_right = lax.ppermute(left, 'gy', [(i + 1, i) for i in range(ny - 1)])]
    unnamed x4 -> x0, other arithmetic: 87.5 us -> none
    ppermute x28 -> x4, waiting for transfers between devices: 26.4 us -> 2.58 us  [the longest x1 2.57 us: per_device(): got_outer = lax.ppermute(jnp.where(even, first, last), 'gx', outer)]
    reshape x6 -> x0, local copies, waits for them, and re-layouts: 19.9 us -> none  [the longest x1 18.6 us: restrict(): residual.reshape(goals, height // COARSEN, COARSEN, width // COARSEN, COA...]
    pallas_call x0 -> x3, Pallas kernels: none -> 17.5 us  [the longest x1 8.32 us: main(): pl.pallas_call(main_kernel, out_shape=jax.ShapeDtypeStruct((GOALS, ROWS,...]
    reduce_sum x2 -> x0, other arithmetic: 9.61 us -> none  [restrict(): return blocks.mean(axis=(2, 4))]
    add x7 -> x0, other arithmetic: 6.84 us -> none  [the longest x1 2.73 us: per_device(): potential = smooth(potential + correction, shifted)]
    mul x14 -> x0, other arithmetic: 6.55 us -> none  [the longest x4 5.46 us: operate_wide(): return diag_wide * field - open_wide * cross_local(open_wide * field)]
  transfers between devices with their start and end apart: 28 -> 4, of which waited for: 10 -> 1; matrix products, arithmetic and copies ran while one was open for 31% -> 0% of each run, Pallas kernels for 0% -> 18%
where the time goes in v1:
time: 42.8 us; the launch traced here: 42.5 us
  starting transfers between devices  20.7 us (48%)
  Pallas kernels  17.5 us (41%)
  waiting for transfers between devices  2.58 us (6%)
  other arithmetic  1.61 us (4%)
    ppermute x1, starting transfers between devices, per_device(): from_right = lax.ppermute(left, 'gy', [(i + 1, i) for i in range(ny - 1)])  9.56 us
    pallas_call x1, Pallas kernels, main(): pl.pallas_call(main_kernel, out_shape=jax.ShapeDtypeStruct((GOALS, ROWS,...  8.32 us
    pallas_call x1, Pallas kernels, exits_of(): pl.pallas_call(exits_kernel, out_shape=jax.ShapeDtypeStruct((GOALS, WIDE,...  7.48 us
    ppermute x1, starting transfers between devices, per_device(): got_outer = lax.ppermute(jnp.where(even, first, last), 'gx', outer)  4.58 us
    ppermute x1, starting transfers between devices, per_device(): from_left = lax.ppermute(right, 'gy', [(i, i + 1) for i in range(ny - 1)])  3.99 us
    ppermute x1, starting transfers between devices, per_device(): got_inner = lax.ppermute(jnp.where(even, last, first), 'gx', inner)  2.58 us
    ppermute x1, waiting for transfers between devices, per_device(): got_outer = lax.ppermute(jnp.where(even, first, last), 'gx', outer)  2.57 us
    pallas_call x1, Pallas kernels, pack(): pl.pallas_call(pack_kernel, out_shape=[jax.ShapeDtypeStruct((8, LANES), F...  1.66 us
  transfers between devices with their start and end apart: 4, of which 1 were waited for; matrix products, arithmetic and copies ran while one was open for 0% of the time, Pallas kernels for 18%

profile of v1, /device:TPU:31, one launch (start us, length us, event | category | flops | bytes accessed | tf_op | source)
XLA Modules:
  0.0 42.5 jit_solution(8340519662849810314)
XLA Ops:
  0.0 1.0 %compare_select_fusion.src_ref = f32[128,256]{1,0:T(8,128)S(1)} fusion(f32[128,256]{1,0:T(8,128)} %param.5, s32[128,256]{1,0:T(8,128)} %param.4), kind=kLoop, calls=%fused_computation | loop fusion | flops 65536 | bytes 393216 | tf_op jit(solution)/shard_map/jit(_where)/select_n | solution.py:302
  1.0 0.0 copy-start
  1.0 2.6 %collective-permute-start.1 = (f32[16,256]{1,0:T(8,128)S(1)}, f32[16,256]{1,0:T(8,128)S(1)}, u32[]{:S(2)}, u32[]{:S(2)}) collective-permute-start(f32[16,256]{1,0:T(8,128)S(1)} %get-tuple-element.9), channel_id=1, source_target_pairs={{0,16},{16,0},{32,48},{48,32},{64,80},{80,64},{96,112},{112,96},{1... | collective-permute-start | bytes 49160 | tf_op jit(solution)/shard_map/ppermute | solution.py:309
  3.6 4.6 %collective-permute-start = (f32[16,256]{1,0:T(8,128)S(1)}, f32[16,256]{1,0:T(8,128)S(1)}, u32[]{:S(2)}, u32[]{:S(2)}) collective-permute-start(f32[16,256]{1,0:T(8,128)S(1)} %get-tuple-element.10), channel_id=1, source_target_pairs={{16,32},{32,16},{48,64},{64,48},{80,96},{96,80},{112,128},{128,112... | collective-permute-start | bytes 49160 | tf_op jit(solution)/shard_map/ppermute | solution.py:308
  8.2 0.0 collective-permute-done.1
  8.2 2.6 %collective-permute-done = f32[16,256]{1,0:T(8,128)S(1)} collective-permute-done((f32[16,256]{1,0:T(8,128)S(1)}, f32[16,256]{1,0:T(8,128)S(1)}, u32[]{:S(2)}, u32[]{:S(2)}) %collective-permute-start) | collective-permute-done | bytes 16416 | tf_op jit(solution)/shard_map/ppermute | solution.py:308
  10.8 0.6 %broadcast_select_fusion = (f32[16,256]{1,0:T(8,128)}, f32[16,256]{1,0:T(8,128)}) fusion(f32[16,256]{1,0:T(8,128)S(1)} %collective-permute-done.1, f32[16,256]{1,0:T(8,128)S(1)} %collective-permute-done, pred[]{:T(512)S(6)} %eq.11), kind=kLoop, calls=%fused_computation.3 | loop fusion | flops 8192 | bytes 65537 | tf_op jit(solution)/shard_map/jit(_where)/select_n | solution.py:312
  11.4 0.0 copy-done
  11.4 0.0 copy-start.4
  11.4 0.0 copy-start.5
  11.4 1.7 %shard_map.46 = (f32[8,384]{1,0:T(8,128)}, f32[8,384]{1,0:T(8,128)}) custom-call(f32[128,256]{1,0:T(8,128)} %copy-done, f32[16,256]{1,0:T(8,128)} %get-tuple-element.12.top_ref, f32[16,256]{1,0:T(8,128)} %get-tuple-element.11.bottom_ref), custom_call_target="tpu_custom_call" | custom-call | tf_op jit(solution)/shard_map/pallas_call | solution.py:124
  13.1 4.0 %collective-permute-start.2 = (f32[8,384]{1,0:T(8,128)}, f32[8,384]{1,0:T(8,128)S(1)}, u32[]{:S(2)}, u32[]{:S(2)}) collective-permute-start(f32[8,384]{1,0:T(8,128)} %get-tuple-element.7), channel_id=1, source_target_pairs={{0,1},{1,2},{2,3},{3,4},{4,5},{5,6},{6,7},{7,8},{8,9},{9,10},{10,1... | collective-permute-start | bytes 36872 | tf_op jit(solution)/shard_map/ppermute | solution.py:314
  17.1 0.0 copy-start.1
  17.1 0.0 copy-start.2
  17.1 0.0 copy-start.3
  17.1 9.6 %collective-permute-start.3 = (f32[8,384]{1,0:T(8,128)}, f32[8,384]{1,0:T(8,128)S(1)}, u32[]{:S(2)}, u32[]{:S(2)}) collective-permute-start(f32[8,384]{1,0:T(8,128)} %get-tuple-element.8), channel_id=1, source_target_pairs={{1,0},{2,1},{3,2},{4,3},{5,4},{6,5},{7,6},{8,7},{9,8},{10,9},{11,1... | collective-permute-start | bytes 36872 | tf_op jit(solution)/shard_map/ppermute | solution.py:315
  26.7 0.0 copy-done.4
  26.7 0.0 copy-done.5
  26.7 7.5 %shard_map.47.exits_ref = f32[4,160,384]{2,1,0:T(8,128)S(1)} custom-call(s32[4,4096]{1,0:T(4,128)S(1)} %copy-done.4, s32[4,4096]{1,0:T(4,128)S(1)} %copy-done.5), custom_call_target="tpu_custom_call" | custom-call | flops 1509949440 | bytes 1048576 | tf_op jit(solution)/shard_map/pallas_call | solution.py:88
  34.2 0.0 collective-permute-done.2.from_left_ref
  34.2 0.0 collective-permute-done.3.from_right_ref
  34.2 0.0 copy-done.1
  34.2 0.0 copy-done.2
  34.2 0.0 copy-done.3
  34.2 8.3 %shard_map.48 = f32[4,128,256]{2,1,0:T(8,128)} custom-call(f32[128,256]{1,0:T(8,128)S(1)} %copy-done.1, f32[16,256]{1,0:T(8,128)S(1)} %copy-done.3, f32[16,256]{1,0:T(8,128)S(1)} %copy-done.2, f32[8,384]{1,0:T(8,128)S(1)} %collective-permute-done.2.from_left_ref, f32[8,384]{1,0:T(8,128)S(1)} %collective-permute-done.3.from_right_ref, ...), custom_call_target="tpu_custom_call" | custom-call | flops 100000000 | bytes 1048576 | tf_op jit(solution)/shard_map/pallas_call | solution.py:285
  (1 shorter events, 0.0 us)
Async XLA Ops:
  1.0 10.4 %copy-start = (f32[128,256]{1,0:T(8,128)}, f32[128,256]{1,0:T(8,128)S(1)}, u32[]{:S(2)}) copy-start(f32[128,256]{1,0:T(8,128)S(1)} %compare_select_fusion.src_ref) | copy-start | bytes 393220
  1.0 7.2 %collective-permute-start.1 = (f32[16,256]{1,0:T(8,128)S(1)}, f32[16,256]{1,0:T(8,128)S(1)}, u32[]{:S(2)}, u32[]{:S(2)}) collective-permute-start(f32[16,256]{1,0:T(8,128)S(1)} %get-tuple-element.9), channel_id=1, source_target_pairs={{0,16},{16,0},{32,48},{48,32},{64,80},{80,64},{96,112},{112,96},{1... | collective-permute-start | bytes 49160 | tf_op jit(solution)/shard_map/ppermute | solution.py:309
  3.6 7.2 %collective-permute-start = (f32[16,256]{1,0:T(8,128)S(1)}, f32[16,256]{1,0:T(8,128)S(1)}, u32[]{:S(2)}, u32[]{:S(2)}) collective-permute-start(f32[16,256]{1,0:T(8,128)S(1)} %get-tuple-element.10), channel_id=1, source_target_pairs={{16,32},{32,16},{48,64},{64,48},{80,96},{96,80},{112,128},{128,112... | collective-permute-start | bytes 49160 | tf_op jit(solution)/shard_map/ppermute | solution.py:308
  11.4 15.3 %copy-start.4 = (s32[4,4096]{1,0:T(4,128)S(1)}, s32[4,4096]{1,0:T(4,128)}, u32[]{:S(2)}) copy-start(s32[4,4096]{1,0:T(4,128)} %rows_ref.1) | copy-start | bytes 196612
  11.4 15.3 %copy-start.5 = (s32[4,4096]{1,0:T(4,128)S(1)}, s32[4,4096]{1,0:T(4,128)}, u32[]{:S(2)}) copy-start(s32[4,4096]{1,0:T(4,128)} %cols_ref.1) | copy-start | bytes 196612
  13.1 21.1 %collective-permute-start.2 = (f32[8,384]{1,0:T(8,128)}, f32[8,384]{1,0:T(8,128)S(1)}, u32[]{:S(2)}, u32[]{:S(2)}) collective-permute-start(f32[8,384]{1,0:T(8,128)} %get-tuple-element.7), channel_id=1, source_target_pairs={{0,1},{1,2},{2,3},{3,4},{4,5},{5,6},{6,7},{7,8},{8,9},{9,10},{10,1... | collective-permute-start | bytes 36872 | tf_op jit(solution)/shard_map/ppermute | solution.py:314
  17.1 17.1 %copy-start.1 = (f32[128,256]{1,0:T(8,128)S(1)}, f32[128,256]{1,0:T(8,128)}, u32[]{:S(2)}) copy-start(f32[128,256]{1,0:T(8,128)} %copy-done) | copy-start | bytes 393220
  17.1 17.1 %copy-start.2 = (f32[16,256]{1,0:T(8,128)S(1)}, f32[16,256]{1,0:T(8,128)}, u32[]{:S(2)}) copy-start(f32[16,256]{1,0:T(8,128)} %get-tuple-element.11.bottom_ref) | copy-start | bytes 49156
  17.1 17.1 %copy-start.3 = (f32[16,256]{1,0:T(8,128)S(1)}, f32[16,256]{1,0:T(8,128)}, u32[]{:S(2)}) copy-start(f32[16,256]{1,0:T(8,128)} %get-tuple-element.12.top_ref) | copy-start | bytes 49156
  17.1 17.1 %collective-permute-start.3 = (f32[8,384]{1,0:T(8,128)}, f32[8,384]{1,0:T(8,128)S(1)}, u32[]{:S(2)}, u32[]{:S(2)}) collective-permute-start(f32[8,384]{1,0:T(8,128)} %get-tuple-element.8), channel_id=1, source_target_pairs={{1,0},{2,1},{3,2},{4,3},{5,4},{6,5},{7,6},{8,7},{9,8},{10,9},{11,1... | collective-permute-start | bytes 36872 | tf_op jit(solution)/shard_map/ppermute | solution.py:315

commit v2 on v1

v2 whole, which is shorter than its diff:
```python
import functools

import jax
import jax.numpy as jnp
import numpy as np
from jax import lax
from jax.experimental import pallas as pl
from jax.experimental.pallas import tpu as pltpu
from jax.sharding import PartitionSpec as P

SCREENING = 0.0001
EXIT_SINK = 4.0
WEIGHT = 4.01
DAMPING = 0.8
CENTER = 6.75
HALF = 5.75

GOALS = 4
ROWS = 128
COLS = 256
HALO = 16
WIDE = ROWS + 2 * HALO
LANES = 384
STEPS = WIDE // 8
CROWS = WIDE // 4
F32 = jnp.float32
BF16 = jnp.bfloat16

COEF = []
_q = CENTER / HALF
_p = 1.0 / _q
for _ in range(3):
    _n = 1.0 / (2.0 * _q - _p)
    COEF.append((_n * _p, 2.0 * _n / HALF))
    _p = _n


def split(x):
    high = x.astype(BF16)
    return high, (x - high.astype(F32)).astype(BF16)


def dot(a, b, dims=((1,), (0,))):
    return lax.dot_general(a, b, (dims, ((), ())), preferred_element_type=F32)


def iota(shape, dim):
    return lax.broadcasted_iota(jnp.int32, shape, dim)


def one_zero(condition):
    return jnp.where(condition, 1.0, 0.0).astype(F32)


def natural(p):
    return STEPS * (p & 7) + (p >> 3)


FAR = 1 << 20


def exits_kernel(rows_ref, cols_ref, out_ref):
    row0 = lax.axis_index("gx") * ROWS - HALO
    col0 = lax.axis_index("gy") * COLS
    count = rows_ref.shape[1] // 128

    keys = []
    for k in range(count):
        r = rows_ref[:, 128 * k : 128 * k + 128] - row0
        c = cols_ref[:, 128 * k : 128 * k + 128] - col0
        near = (r >= 0) & (r < WIDE) & (c >= -HALO) & (c < COLS + HALO)
        c = jnp.where(c < 0, c + COLS + HALO, jnp.where(c >= COLS, c + HALO, c))
        keys.append(jnp.where(near, r * 512 + c, FAR))

    def take(keys):
        least = functools.reduce(jnp.minimum, keys)
        return least, [jnp.where(k == least, FAR, k) for k in keys]

    row_at = natural(iota((WIDE, 256), 0))
    col_at = iota((COLS + 2 * HALO, 256), 0)

    def marks(g, one, two):
        key = jnp.concatenate([one[g : g + 1], two[g : g + 1]], axis=1)
        left = one_zero(row_at == (key >> 9)).astype(BF16)
        right = one_zero(col_at == (key & 511)).astype(BF16)
        return dot(left, right, ((1,), (1,)))

    def put(g, total):
        sink = jnp.minimum(total, 1.0) * EXIT_SINK
        out_ref[g, :, 0:COLS] = sink[:, :COLS]
        tail = jnp.concatenate([sink[:, COLS:], jnp.zeros((WIDE, 128 - 2 * HALO), F32)], axis=1)
        out_ref[g, :, COLS:LANES] = pltpu.roll(tail, 128 - HALO, 1)

    one, keys = take(keys)
    two, keys = take(keys)
    for g in range(GOALS):
        put(g, marks(g, one, two))

    def more(keys):
        return jnp.min(functools.reduce(jnp.minimum, keys)) < FAR

    def again(keys):
        one, keys = take(keys)
        two, keys = take(keys)
        for g in range(GOALS):
            extra = jnp.minimum(marks(g, one, two), 1.0) * EXIT_SINK
            out_ref[g, :, 0:COLS] = jnp.maximum(out_ref[g, :, 0:COLS], extra[:, :COLS])
            tail = jnp.concatenate([extra[:, COLS:], jnp.zeros((WIDE, 128 - 2 * HALO), F32)], axis=1)
            out_ref[g, :, COLS:LANES] = jnp.maximum(out_ref[g, :, COLS:LANES], pltpu.roll(tail, 128 - HALO, 1))
        return keys

    lax.while_loop(more, again, keys)


def exits_of(rows, cols):
    return pl.pallas_call(
        exits_kernel,
        out_shape=jax.ShapeDtypeStruct((GOALS, WIDE, LANES), F32),
        in_specs=[pl.BlockSpec(memory_space=pltpu.VMEM)] * 2,
        out_specs=pl.BlockSpec(memory_space=pltpu.VMEM),
        compiler_params=pltpu.CompilerParams(vmem_limit_bytes=8 * 2**20),
        cost_estimate=pl.CostEstimate(flops=2 * 4 * 256 * 160 * 288, bytes_accessed=2**20, transcendentals=0),
    )(rows, cols)


def pack_kernel(src_ref, outer_ref, inner_ref, left_ref, right_ref, top_ref, bottom_ref):
    even = lax.rem(lax.axis_index("gx"), 2) == 0
    top_ref[...] = jnp.where(even, outer_ref[...], inner_ref[...])
    bottom_ref[...] = jnp.where(even, inner_ref[...], outer_ref[...])

    def tile(q, lo):
        if q < HALO // 8:
            return top_ref[8 * q : 8 * q + 8, lo : lo + 128]
        if q >= (HALO + ROWS) // 8:
            at = 8 * q - HALO - ROWS
            return bottom_ref[at : at + 8, lo : lo + 128]
        at = 8 * q - HALO
        return src_ref[at : at + 8, lo : lo + 128]

    lane = iota((8, 128), 1)
    for b in range(LANES // 128):
        left = jnp.zeros((8, 128), F32)
        right = jnp.zeros((8, 128), F32)
        for m in range(8):
            q = 8 * b + m
            if q >= WIDE // 8:
                break
            here = (lane >= HALO * m) & (lane < HALO * (m + 1))
            left = jnp.where(here, pltpu.roll(tile(q, 0), HALO * m, 1), left)
            right = jnp.where(here, pltpu.roll(tile(q, COLS - 128), (HALO * m + HALO) % 128, 1), right)
        left_ref[:, 128 * b : 128 * b + 128] = left
        right_ref[:, 128 * b : 128 * b + 128] = right


def pack(src, outer, inner):
    return pl.pallas_call(
        pack_kernel,
        out_shape=[jax.ShapeDtypeStruct((8, LANES), F32)] * 2 + [jax.ShapeDtypeStruct((HALO, COLS), F32)] * 2,
        in_specs=[pl.BlockSpec(memory_space=pltpu.VMEM)] * 3,
        out_specs=[pl.BlockSpec(memory_space=pltpu.VMEM)] * 4,
        compiler_params=pltpu.CompilerParams(vmem_limit_bytes=4 * 2**20),
    )(src, outer, inner)


def main_kernel(
    src_ref, top_ref, bottom_ref, from_left_ref, from_right_ref, exits_ref, out_ref,
    nat_ref, s_ref, o_ref, diag_ref, r1_ref, corr_ref, shift_ref, dg_ref, da_ref, db_ref, r_ref, x_ref, y_ref, pool_ref, grow_ref,
):
    gx, gy = lax.axis_index("gx"), lax.axis_index("gy")

    for b in range(COLS // 128):
        at = slice(128 * b, 128 * b + 128)
        nat_ref[b, 0:HALO, :] = top_ref[:, at]
        nat_ref[b, HALO : HALO + ROWS, :] = src_ref[:, at]
        nat_ref[b, HALO + ROWS : WIDE, :] = bottom_ref[:, at]
    lane = iota((8, 128), 1)
    for q in range(STEPS):
        b, m = divmod(q, 8)
        at = slice(128 * b, 128 * b + 128)
        ahead = pltpu.roll(from_right_ref[:, at], (128 - HALO * m) % 128, 1)
        behind = pltpu.roll(from_left_ref[:, at], (128 - HALO - HALO * m) % 128, 1)
        both = jnp.where(lane < HALO, ahead, jnp.where(lane >= 128 - HALO, behind, 0.0))
        nat_ref[COLS // 128, 8 * q : 8 * q + 8, :] = both

    def ends(ref, first, last):
        ref[0] = pltpu.roll(last, 1, 0)
        ref[STEPS + 1] = pltpu.roll(first, 7, 0)

    def sweep(ref, body):
        before, mid = ref[0], ref[1]
        results = []
        for t in range(STEPS):
            after = ref[t + 2]
            beside = pltpu.roll(mid, LANES - 1, 1) + pltpu.roll(mid, 1, 1)
            results.append(body(t, mid, (after + before) + beside))
            before, mid = mid, after
        return results[0], results[-1]

    for t in range(STEPS):
        s = jnp.concatenate([nat_ref[b, pl.ds(t, 8, stride=STEPS), :] for b in range(LANES // 128)], axis=1)
        o = one_zero(s > 0.0)
        s_ref[t + 1] = s
        o_ref[t + 1] = o
    ends(s_ref, s_ref[1], s_ref[STEPS])
    ends(o_ref, o_ref[1], o_ref[STEPS])

    def first_diag(t, o, cross):
        diag_ref[t] = SCREENING + 4.0 * (1.0 - o) + o * cross

    sweep(o_ref, first_diag)

    def first_r(t, s, cross):
        r1_ref[t] = s - diag_ref[t] * (s * (1.0 / CENTER)) + o_ref[t + 1] * (cross * (1.0 / CENTER))

    sweep(s_ref, first_r)

    fine_col, coarse_col = iota((LANES, 128), 0), iota((LANES, 128), 1)
    fine_col = jnp.where(fine_col >= 320, fine_col - LANES, fine_col)
    coarse_col = jnp.where(coarse_col >= 96, coarse_col - 128, coarse_col)
    gather_cols = jnp.where((fine_col >> 2) == coarse_col, 0.25, 0.0).astype(BF16)
    fine_row, coarse_row = natural(iota((CROWS, WIDE), 1)), iota((CROWS, WIDE), 0)
    gather_rows = jnp.where((fine_row >> 2) == coarse_row, 0.25, 0.0).astype(BF16)
    gather_rows = jnp.concatenate([gather_rows, gather_rows], axis=1)
    spread_c, spread_f = iota((256, LANES), 0) & 127, iota((256, LANES), 1)
    spread_c = jnp.where(spread_c >= 96, spread_c - 128, spread_c)
    spread_f = jnp.where(spread_f >= 320, spread_f - LANES, spread_f)
    spread_cols = one_zero(spread_c == (spread_f >> 2)).astype(BF16)

    def spread_of(fine):
        c = iota(fine.shape, 1)
        c = jnp.where(c >= CROWS, c - CROWS, c)
        return one_zero((fine >> 2) == c).astype(BF16)

    def restrict(field):
        high, low = split(field)
        part = dot(high, gather_cols) + dot(low, gather_cols)
        high, low = split(part)
        return dot(gather_rows, jnp.concatenate([high, low], axis=0))

    def prolong_cols(e):
        high, low = split(e)
        return dot(jnp.concatenate([high, low], axis=1), spread_cols)

    def prolong_rows(e, spread):
        high, low = split(e)
        return dot(spread, jnp.concatenate([high, low], axis=0))

    def coarse(f):
        n = f.shape[0]
        row = gx * (ROWS // 4) + (lax.rem(iota((n, 128), 0), CROWS) - HALO // 4)
        col = iota((n, 128), 1)
        col = gy * (COLS // 4) + jnp.where(col >= 96, col - 128, col)
        inside = (row >= 0) & (row < 32 * (ROWS // 4)) & (col >= 0) & (col < 16 * (COLS // 4))
        mask = one_zero(inside)
        f = f * (DAMPING / WEIGHT)
        e = f * mask
        for _ in range(3):
            cr = (pltpu.roll(e, n - 1, 0) + pltpu.roll(e, 1, 0)) + (pltpu.roll(e, 127, 1) + pltpu.roll(e, 1, 1))
            e = ((1.0 - DAMPING) * e + f + (DAMPING / WEIGHT) * cr) * mask
        return e

    estimate = coarse(restrict(s_ref[1 : STEPS + 1].reshape(WIDE, LANES)))
    wide = prolong_rows(prolong_cols(estimate), spread_of(natural(iota((WIDE, 2 * CROWS), 0))))
    for t in range(STEPS):
        corr_ref[t + 1] = wide[8 * t : 8 * t + 8] * o_ref[t + 1]
    ends(corr_ref, corr_ref[1], corr_ref[STEPS])

    def first_shift(t, c, cross):
        shift_ref[t] = o_ref[t + 1] * cross - diag_ref[t] * c

    sweep(corr_ref, first_shift)

    (a1, b1), (a2, b2), (a3, b3) = COEF

    def goal(g, carry):
        def advance(old_ref, new_ref, a, b, also=None):
            def body(t, mid, cross):
                r = r_ref[t] - dg_ref[t] * mid + o_ref[t + 1] * cross
                d = a * mid + b * r
                r_ref[t] = r
                new_ref[t + 1] = d
                if also is not None:
                    also(t, mid, d)
                return d

            ends(new_ref, *sweep(old_ref, body))

        new = []
        for t in range(STEPS):
            s = s_ref[t + 1]
            hit = o_ref[t + 1] * exits_ref[g, 8 * t : 8 * t + 8, :]
            d = s * (1.0 / CENTER)
            r = r1_ref[t] - hit * d
            n = a1 * d + b1 * r
            dg_ref[t] = diag_ref[t] + hit
            r_ref[t] = r
            da_ref[t + 1] = n
            new.append(n)
        ends(da_ref, new[0], new[-1])

        def sum_1(t, mid, d):
            x_ref[g, t] = s_ref[t + 1, :, 0:COLS] * (1.0 / CENTER) + mid[:, :COLS] + d[:, :COLS]

        advance(da_ref, db_ref, a2, b2, sum_1)
        advance(db_ref, da_ref, a3, b3)

        def middle(t, mid, cross):
            o, c = o_ref[t + 1], corr_ref[t + 1]
            dg = dg_ref[t]
            r = r_ref[t] - dg * mid + o * cross
            pool_ref[t] = r
            r = r + shift_ref[t] - (dg - diag_ref[t]) * c
            d = r * (1.0 / CENTER)
            r_ref[t] = r
            db_ref[t + 1] = d
            x_ref[g, t] += (mid + c + d)[:, :COLS]
            return d

        ends(db_ref, *sweep(da_ref, middle))
        grow_ref[g] = restrict(pool_ref[...].reshape(WIDE, LANES))
        advance(db_ref, da_ref, a1, b1)

        def sum_2(t, mid, d):
            x_ref[g, t] += mid[:, :COLS] + d[:, :COLS]

        advance(da_ref, db_ref, a2, b2, sum_2)

        def last(t, mid, cross):
            r = r_ref[t] - dg_ref[t] * mid + o_ref[t + 1] * cross
            y = x_ref[g, t] + (a3 * mid + b3 * r)[:, :COLS]
            for b in range(COLS // 128):
                y_ref[g, b, pl.ds(t, 8, stride=STEPS), :] = y[:, 128 * b : 128 * b + 128]

        sweep(db_ref, last)
        return carry

    lax.fori_loop(0, GOALS, goal, 0)

    after = coarse(grow_ref[...].reshape(GOALS * CROWS, 128))
    wide = prolong_cols(after)
    spread = spread_of(iota((ROWS, 2 * CROWS), 0) + HALO)
    o = one_zero(src_ref[...] > 0.0)
    for g in range(GOALS):
        add = prolong_rows(wide[g * CROWS : (g + 1) * CROWS, 0:COLS], spread)
        add = o * add
        for b in range(COLS // 128):
            at = slice(128 * b, 128 * b + 128)
            out_ref[g, :, at] = y_ref[g, b, HALO : HALO + ROWS, :] + add[:, at]


def main(src, top, bottom, from_left, from_right, exits):
    padded = pltpu.VMEM((STEPS + 2, 8, LANES), F32)
    plain = pltpu.VMEM((STEPS, 8, LANES), F32)
    return pl.pallas_call(
        main_kernel,
        out_shape=jax.ShapeDtypeStruct((GOALS, ROWS, COLS), F32),
        in_specs=[pl.BlockSpec(memory_space=pltpu.VMEM)] * 6,
        out_specs=pl.BlockSpec(memory_space=pltpu.VMEM),
        scratch_shapes=[
            pltpu.VMEM((LANES // 128, WIDE, 128), F32), padded, padded, plain, plain, padded, plain, plain, padded, padded, plain,
            pltpu.VMEM((GOALS, STEPS, 8, COLS), F32), pltpu.VMEM((GOALS, COLS // 128, WIDE, 128), F32), plain,
            pltpu.VMEM((GOALS, CROWS, 128), F32),
        ],
        compiler_params=pltpu.CompilerParams(vmem_limit_bytes=16 * 2**20),
        cost_estimate=pl.CostEstimate(flops=10**8, bytes_accessed=2**20, transcendentals=0),
    )(src, top, bottom, from_left, from_right, exits)


def per_device(obstacles, load, exit_rows, exit_cols):
    gx, gy = lax.axis_index("gx"), lax.axis_index("gy")
    ny = lax.axis_size("gy")
    source = jnp.where(obstacles == 0, load, 0.0)
    first, last = source[:HALO], source[ROWS - HALO :]
    even = lax.rem(gx, 2) == 0
    nx = lax.axis_size("gx")
    inner = [(i, i ^ 1) for i in range(nx)]
    outer = [(i, j) for i in range(1, nx - 1) for j in [((i + 1) ^ 1) - 1]]
    got_outer = lax.ppermute(jnp.where(even, first, last), "gx", outer)
    got_inner = lax.ppermute(jnp.where(even, last, first), "gx", inner)
    exits = exits_of(exit_rows, exit_cols)
    left, right, top, bottom = pack(source, got_outer, got_inner)
    from_left = lax.ppermute(right, "gy", [(i, i + 1) for i in range(ny - 1)])
    from_right = lax.ppermute(left, "gy", [(i + 1, i) for i in range(ny - 1)])
    return main(source, top, bottom, from_left, from_right, exits)


def solution(mesh):
    in_specs = (P("gx", "gy"), P("gx", "gy"), P(), P())
    out_specs = P(None, "gx", "gy")
    return jax.shard_map(
        per_device, mesh=mesh, in_specs=in_specs, out_specs=out_specs, check_vma=False
    )
```

time: 42.8 us -> 32.1 us (0.75)
  Pallas kernels: 17.5 us -> 7.47 us
  other arithmetic: 1.61 us -> 0.99 us
    pallas_call x1, Pallas kernels: 7.48 us -> 0.79 us  [exits_of(): pl.pallas_call(exits_kernel, out_shape=jax.ShapeDtypeStruct((GOALS, WIDE,...]
    pallas_call x1, Pallas kernels: 8.32 us -> 6.57 us  [main(): pl.pallas_call(main_kernel, out_shape=jax.ShapeDtypeStruct((GOALS, ROWS,...]
    pallas_call x1, Pallas kernels: 1.66 us -> 0.1 us  [pack(): pl.pallas_call(pack_kernel, out_shape=[jax.ShapeDtypeStruct((8, LANES), F...]
    select_n x1 -> x0, other arithmetic: 0.62 us -> none  [per_device(): bottom = jnp.where(even, got_inner, got_outer)]
  transfers between devices with their start and end apart: 4 -> 4, of which waited for: 1 -> 1; matrix products, arithmetic and copies ran while one was open for 0% -> 0% of each run, Pallas kernels for 18% -> 2%
where the time goes in v2:
time: 32.1 us; the launch traced here: 31.9 us
  starting transfers between devices  20.7 us (64%)
  Pallas kernels  7.47 us (23%)
  waiting for transfers between devices  2.58 us (8%)
  other arithmetic  0.99 us (3%)
    ppermute x1, starting transfers between devices, per_device(): from_right = lax.ppermute(left, 'gy', [(i + 1, i) for i in range(ny - 1)])  9.43 us
    pallas_call x1, Pallas kernels, main(): pl.pallas_call(main_kernel, out_shape=jax.ShapeDtypeStruct((GOALS, ROWS,...  6.57 us
    ppermute x1, starting transfers between devices, per_device(): got_outer = lax.ppermute(jnp.where(even, first, last), 'gx', outer)  4.71 us
    ppermute x1, starting transfers between devices, per_device(): from_left = lax.ppermute(right, 'gy', [(i, i + 1) for i in range(ny - 1)])  4 us
    ppermute x1, starting transfers between devices, per_device(): got_inner = lax.ppermute(jnp.where(even, last, first), 'gx', inner)  2.58 us
    ppermute x1, waiting for transfers between devices, per_device(): got_outer = lax.ppermute(jnp.where(even, first, last), 'gx', outer)  2.57 us
    select_n x1, other arithmetic, per_device(): source = jnp.where(obstacles == 0, load, 0.0)  0.98 us
    pallas_call x1, Pallas kernels, exits_of(): pl.pallas_call(exits_kernel, out_shape=jax.ShapeDtypeStruct((GOALS, WIDE,...  0.79 us
  transfers between devices with their start and end apart: 4, of which 1 were waited for; matrix products, arithmetic and copies ran while one was open for 0% of the time, Pallas kernels for 2%

profile of v2, /device:TPU:31, one launch (start us, length us, event | category | flops | bytes accessed | tf_op | source)
XLA Modules:
  0.0 31.9 jit_solution(3988096496564279308)
XLA Ops:
  0.0 1.0 %compare_select_fusion.src_ref = f32[128,256]{1,0:T(8,128)S(1)} fusion(f32[128,256]{1,0:T(8,128)} %param.5, s32[128,256]{1,0:T(8,128)} %param.4), kind=kLoop, calls=%fused_computation | loop fusion | flops 65536 | bytes 393216 | tf_op jit(solution)/shard_map/jit(_where)/select_n | solution.py:372
  1.0 2.6 %collective-permute-start.1 = (f32[16,256]{1,0:T(8,128)S(1)}, f32[16,256]{1,0:T(8,128)S(1)}, u32[]{:S(2)}, u32[]{:S(2)}) collective-permute-start(f32[16,256]{1,0:T(8,128)S(1)} %get-tuple-element.13), channel_id=1, source_target_pairs={{0,16},{16,0},{32,48},{48,32},{64,80},{80,64},{96,112},{112,96},{1... | collective-permute-start | bytes 49160 | tf_op jit(solution)/shard_map/ppermute | solution.py:379
  3.6 0.0 copy-start
  3.6 0.0 copy-start.1
  3.6 4.7 %collective-permute-start = (f32[16,256]{1,0:T(8,128)S(1)}, f32[16,256]{1,0:T(8,128)S(1)}, u32[]{:S(2)}, u32[]{:S(2)}) collective-permute-start(f32[16,256]{1,0:T(8,128)S(1)} %get-tuple-element.14), channel_id=1, source_target_pairs={{16,32},{32,16},{48,64},{64,48},{80,96},{96,80},{112,128},{128,112... | collective-permute-start | bytes 49160 | tf_op jit(solution)/shard_map/ppermute | solution.py:378
  8.3 0.0 collective-permute-done.1.inner_ref
  8.3 2.6 %collective-permute-done.outer_ref = f32[16,256]{1,0:T(8,128)S(1)} collective-permute-done((f32[16,256]{1,0:T(8,128)S(1)}, f32[16,256]{1,0:T(8,128)S(1)}, u32[]{:S(2)}, u32[]{:S(2)}) %collective-permute-start) | collective-permute-done | bytes 16416 | tf_op jit(solution)/shard_map/ppermute | solution.py:378
  10.9 0.1 shard_map.46
  11.0 4.0 %collective-permute-start.2 = (f32[8,384]{1,0:T(8,128)S(1)}, f32[8,384]{1,0:T(8,128)S(1)}, u32[]{:S(2)}, u32[]{:S(2)}) collective-permute-start(f32[8,384]{1,0:T(8,128)S(1)} %get-tuple-element.11), channel_id=1, source_target_pairs={{0,1},{1,2},{2,3},{3,4},{4,5},{5,6},{6,7},{7,8},{8,9},{9,10},{10,1... | collective-permute-start | bytes 36872 | tf_op jit(solution)/shard_map/ppermute | solution.py:382
  15.0 9.4 %collective-permute-start.3 = (f32[8,384]{1,0:T(8,128)S(1)}, f32[8,384]{1,0:T(8,128)S(1)}, u32[]{:S(2)}, u32[]{:S(2)}) collective-permute-start(f32[8,384]{1,0:T(8,128)S(1)} %get-tuple-element.12), channel_id=1, source_target_pairs={{1,0},{2,1},{3,2},{4,3},{5,4},{6,5},{7,6},{8,7},{9,8},{10,9},{11,1... | collective-permute-start | bytes 36872 | tf_op jit(solution)/shard_map/ppermute | solution.py:383
  24.5 0.0 copy-done
  24.5 0.0 copy-done.1
  24.5 0.8 %shard_map.47.exits_ref = f32[4,160,384]{2,1,0:T(8,128)S(1)} custom-call(s32[4,4096]{1,0:T(4,128)S(1)} %copy-done, s32[4,4096]{1,0:T(4,128)S(1)} %copy-done.1), custom_call_target="tpu_custom_call" | custom-call | flops 94371840 | bytes 1048576 | tf_op jit(solution)/shard_map/pallas_call | solution.py:116
  25.3 0.0 collective-permute-done.2.from_left_ref
  25.3 0.0 collective-permute-done.3.from_right_ref
  25.3 6.6 %shard_map.48 = f32[4,128,256]{2,1,0:T(8,128)} custom-call(f32[128,256]{1,0:T(8,128)S(1)} %compare_select_fusion.src_ref, f32[16,256]{1,0:T(8,128)S(1)} %get-tuple-element.9.top_ref, f32[16,256]{1,0:T(8,128)S(1)} %get-tuple-element.10.bottom_ref, f32[8,384]{1,0:T(8,128)S(1)} %collective-permute-done.2.from_left_ref, ...), custom_call_target="tpu_custom_call" | custom-call | flops 100000000 | bytes 1048576 | tf_op jit(solution)/shard_map/pallas_call | solution.py:354
  (1 shorter events, 0.0 us)
Async XLA Ops:
  1.0 7.3 %collective-permute-start.1 = (f32[16,256]{1,0:T(8,128)S(1)}, f32[16,256]{1,0:T(8,128)S(1)}, u32[]{:S(2)}, u32[]{:S(2)}) collective-permute-start(f32[16,256]{1,0:T(8,128)S(1)} %get-tuple-element.13), channel_id=1, source_target_pairs={{0,16},{16,0},{32,48},{48,32},{64,80},{80,64},{96,112},{112,96},{1... | collective-permute-start | bytes 49160 | tf_op jit(solution)/shard_map/ppermute | solution.py:379
  3.6 20.9 %copy-start = (s32[4,4096]{1,0:T(4,128)S(1)}, s32[4,4096]{1,0:T(4,128)}, u32[]{:S(2)}) copy-start(s32[4,4096]{1,0:T(4,128)} %rows_ref.1) | copy-start | bytes 196612
  3.6 20.9 %copy-start.1 = (s32[4,4096]{1,0:T(4,128)S(1)}, s32[4,4096]{1,0:T(4,128)}, u32[]{:S(2)}) copy-start(s32[4,4096]{1,0:T(4,128)} %cols_ref.1) | copy-start | bytes 196612
  3.6 7.3 %collective-permute-start = (f32[16,256]{1,0:T(8,128)S(1)}, f32[16,256]{1,0:T(8,128)S(1)}, u32[]{:S(2)}, u32[]{:S(2)}) collective-permute-start(f32[16,256]{1,0:T(8,128)S(1)} %get-tuple-element.14), channel_id=1, source_target_pairs={{16,32},{32,16},{48,64},{64,48},{80,96},{96,80},{112,128},{128,112... | collective-permute-start | bytes 49160 | tf_op jit(solution)/shard_map/ppermute | solution.py:378
  11.0 14.3 %collective-permute-start.2 = (f32[8,384]{1,0:T(8,128)S(1)}, f32[8,384]{1,0:T(8,128)S(1)}, u32[]{:S(2)}, u32[]{:S(2)}) collective-permute-start(f32[8,384]{1,0:T(8,128)S(1)} %get-tuple-element.11), channel_id=1, source_target_pairs={{0,1},{1,2},{2,3},{3,4},{4,5},{5,6},{6,7},{7,8},{8,9},{9,10},{10,1... | collective-permute-start | bytes 36872 | tf_op jit(solution)/shard_map/ppermute | solution.py:382
  15.0 10.3 %collective-permute-start.3 = (f32[8,384]{1,0:T(8,128)S(1)}, f32[8,384]{1,0:T(8,128)S(1)}, u32[]{:S(2)}, u32[]{:S(2)}) collective-permute-start(f32[8,384]{1,0:T(8,128)S(1)} %get-tuple-element.12), channel_id=1, source_target_pairs={{1,0},{2,1},{3,2},{4,3},{5,4},{6,5},{7,6},{8,7},{9,8},{10,9},{11,1... | collective-permute-start | bytes 36872 | tf_op jit(solution)/shard_map/ppermute | solution.py:383

commit v3 on v2

v3 whole, which is shorter than its diff:
```python
import functools

import jax
import jax.numpy as jnp
import numpy as np
from jax import lax
from jax.experimental import pallas as pl
from jax.experimental.pallas import tpu as pltpu
from jax.sharding import PartitionSpec as P

SCREENING = 0.0001
EXIT_SINK = 4.0
WEIGHT = 4.01
DAMPING = 0.8
CENTER = 6.75
HALF = 5.75

GOALS = 4
ROWS = 128
COLS = 256
HALO = 16
WIDE = ROWS + 2 * HALO
STRIP = WIDE * HALO // 8 + 64
FRINGE = 128
KEPT = FRINGE // 2 - HALO
STEPS = WIDE // 8
CROWS = WIDE // 4
F32 = jnp.float32
BF16 = jnp.bfloat16

COEF = []
_q = CENTER / HALF
_p = 1.0 / _q
for _ in range(3):
    _n = 1.0 / (2.0 * _q - _p)
    COEF.append((_n * _p, 2.0 * _n / HALF))
    _p = _n


def split(x):
    high = x.astype(BF16)
    return high, (x - high.astype(F32)).astype(BF16)


def dot(a, b, dims=((1,), (0,))):
    return lax.dot_general(a, b, (dims, ((), ())), preferred_element_type=F32)


def iota(shape, dim):
    return lax.broadcasted_iota(jnp.int32, shape, dim)


def one_zero(condition):
    return jnp.where(condition, 1.0, 0.0).astype(F32)


def natural(p):
    return STEPS * (p & 7) + (p >> 3)


FAR = 1 << 20


def mark_exits(rows_ref, cols_ref, inner_ref, fringe_ref):
    row0 = lax.axis_index("gx") * ROWS - HALO
    col0 = lax.axis_index("gy") * COLS - HALO
    keys = []
    for k in range(rows_ref.shape[1] // 128):
        r = rows_ref[:, 128 * k : 128 * k + 128] - row0
        c = cols_ref[:, 128 * k : 128 * k + 128] - col0
        near = (r >= 0) & (r < WIDE) & (c >= 0) & (c < COLS + 2 * HALO)
        keys.append(jnp.where(near, r * 512 + c, FAR))

    def take(keys):
        least = functools.reduce(jnp.minimum, keys)
        return least, [jnp.where(k == least, FAR, k) for k in keys]

    row_at = natural(iota((WIDE, 256), 0))
    inner_at = iota((COLS, 256), 0) + HALO
    fringe_at = iota((FRINGE, 256), 0)
    fringe_at = jnp.where(fringe_at < FRINGE // 2, fringe_at, fringe_at + (COLS + 2 * HALO - FRINGE))

    def marks(g, one, two):
        key = jnp.concatenate([one[g : g + 1], two[g : g + 1]], axis=1)
        at_row = one_zero(row_at == (key >> 9)).astype(BF16)
        col = key & 511
        for ref, at in ((inner_ref, inner_at), (fringe_ref, fringe_at)):
            count = dot(at_row, one_zero(at == col).astype(BF16), ((1,), (1,)))
            yield ref, jnp.minimum(count, 1.0) * EXIT_SINK

    one, keys = take(keys)
    two, keys = take(keys)
    for g in range(GOALS):
        for ref, sink in marks(g, one, two):
            ref[g] = sink

    def more(keys):
        return jnp.min(functools.reduce(jnp.minimum, keys)) < FAR

    def again(keys):
        one, keys = take(keys)
        two, keys = take(keys)
        for g in range(GOALS):
            for ref, sink in marks(g, one, two):
                ref[g] = jnp.maximum(ref[g], sink)
        return keys

    lax.while_loop(more, again, keys)


def run_cycles(width, column, nat_ref, exits_ref, scratch, finish):
    s_ref, o_ref, diag_ref, r1_ref, corr_ref, shift_ref, dg_ref, da_ref, db_ref, r_ref, x_ref, y_ref, pool_ref, grow_ref = scratch
    gx, gy = lax.axis_index("gx"), lax.axis_index("gy")
    tiles = range(width // 128)

    def ends(ref, first, last):
        ref[0] = pltpu.roll(last, 1, 0)
        ref[STEPS + 1] = pltpu.roll(first, 7, 0)

    def sweep(ref, body):
        before, mid = ref[0], ref[1]
        results = []
        for t in range(STEPS):
            after = ref[t + 2]
            beside = pltpu.roll(mid, width - 1, 1) + pltpu.roll(mid, 1, 1)
            results.append(body(t, mid, (after + before) + beside))
            before, mid = mid, after
        return results[0], results[-1]

    for t in range(STEPS):
        s = jnp.concatenate([nat_ref[b, pl.ds(t, 8, stride=STEPS), :] for b in tiles], axis=1)
        s_ref[t + 1] = s
        o_ref[t + 1] = one_zero(s > 0.0)
    ends(s_ref, s_ref[1], s_ref[STEPS])
    ends(o_ref, o_ref[1], o_ref[STEPS])

    def first_diag(t, o, cross):
        diag_ref[t] = SCREENING + 4.0 * (1.0 - o) + o * cross

    sweep(o_ref, first_diag)

    def first_r(t, s, cross):
        r1_ref[t] = s - diag_ref[t] * (s * (1.0 / CENTER)) + o_ref[t + 1] * (cross * (1.0 / CENTER))

    sweep(s_ref, first_r)

    gather_cols = jnp.where((iota((width, 128), 0) >> 2) == iota((width, 128), 1), 0.25, 0.0).astype(BF16)
    gather_rows = jnp.where((natural(iota((CROWS, WIDE), 1)) >> 2) == iota((CROWS, WIDE), 0), 0.25, 0.0).astype(BF16)
    gather_rows = jnp.concatenate([gather_rows, gather_rows], axis=1)
    spread_cols = one_zero((iota((256, width), 0) & 127) == (iota((256, width), 1) >> 2)).astype(BF16)

    def spread_of(fine):
        c = iota(fine.shape, 1)
        c = jnp.where(c >= CROWS, c - CROWS, c)
        return one_zero((fine >> 2) == c).astype(BF16)

    def restrict(field):
        high, low = split(field)
        part = dot(high, gather_cols) + dot(low, gather_cols)
        high, low = split(part)
        return dot(gather_rows, jnp.concatenate([high, low], axis=0))

    def prolong_cols(e):
        high, low = split(e)
        return dot(jnp.concatenate([high, low], axis=1), spread_cols)

    def prolong_rows(e, spread):
        high, low = split(e)
        return dot(spread, jnp.concatenate([high, low], axis=0))

    def coarse(f):
        n = f.shape[0]
        row = gx * (ROWS // 4) + (lax.rem(iota((n, 128), 0), CROWS) - HALO // 4)
        lane = iota((n, 128), 1)
        col = gy * (COLS // 4) + column(lane)
        inside = (row >= 0) & (row < 32 * (ROWS // 4)) & (col >= 0) & (col < 16 * (COLS // 4)) & (lane < width // 4)
        mask = one_zero(inside)
        f = f * (DAMPING / WEIGHT)
        e = f * mask
        for _ in range(3):
            cr = (pltpu.roll(e, n - 1, 0) + pltpu.roll(e, 1, 0)) + (pltpu.roll(e, 127, 1) + pltpu.roll(e, 1, 1))
            e = ((1.0 - DAMPING) * e + f + (DAMPING / WEIGHT) * cr) * mask
        return e

    estimate = coarse(restrict(s_ref[1 : STEPS + 1].reshape(WIDE, width)))
    wide = prolong_rows(prolong_cols(estimate), spread_of(natural(iota((WIDE, 2 * CROWS), 0))))
    for t in range(STEPS):
        corr_ref[t + 1] = wide[8 * t : 8 * t + 8] * o_ref[t + 1]
    ends(corr_ref, corr_ref[1], corr_ref[STEPS])

    def first_shift(t, c, cross):
        shift_ref[t] = o_ref[t + 1] * cross - diag_ref[t] * c

    sweep(corr_ref, first_shift)

    (a1, b1), (a2, b2), (a3, b3) = COEF

    for g in range(GOALS):

        def advance(old_ref, new_ref, a, b, also=None):
            def body(t, mid, cross):
                r = r_ref[t] - dg_ref[t] * mid + o_ref[t + 1] * cross
                d = a * mid + b * r
                r_ref[t] = r
                new_ref[t + 1] = d
                if also is not None:
                    also(t, mid, d)
                return d

            ends(new_ref, *sweep(old_ref, body))

        new = []
        for t in range(STEPS):
            hit = o_ref[t + 1] * exits_ref[g, 8 * t : 8 * t + 8, :]
            d = s_ref[t + 1] * (1.0 / CENTER)
            r = r1_ref[t] - hit * d
            n = a1 * d + b1 * r
            dg_ref[t] = diag_ref[t] + hit
            r_ref[t] = r
            da_ref[t + 1] = n
            new.append(n)
        ends(da_ref, new[0], new[-1])

        def sum_1(t, mid, d):
            x_ref[t] = s_ref[t + 1] * (1.0 / CENTER) + mid + d

        advance(da_ref, db_ref, a2, b2, sum_1)
        advance(db_ref, da_ref, a3, b3)

        def middle(t, mid, cross):
            o, c = o_ref[t + 1], corr_ref[t + 1]
            dg = dg_ref[t]
            r = r_ref[t] - dg * mid + o * cross
            pool_ref[t] = r
            r = r + shift_ref[t] - (dg - diag_ref[t]) * c
            d = r * (1.0 / CENTER)
            r_ref[t] = r
            db_ref[t + 1] = d
            x_ref[t] += mid + c + d
            return d

        ends(db_ref, *sweep(da_ref, middle))
        grow_ref[g] = restrict(pool_ref[...].reshape(WIDE, width))
        advance(db_ref, da_ref, a1, b1)

        def sum_2(t, mid, d):
            x_ref[t] += mid + d

        advance(da_ref, db_ref, a2, b2, sum_2)

        def last(t, mid, cross):
            r = r_ref[t] - dg_ref[t] * mid + o_ref[t + 1] * cross
            y = x_ref[t] + (a3 * mid + b3 * r)
            for b in tiles:
                y_ref[g, b, pl.ds(t, 8, stride=STEPS), :] = y[:, 128 * b : 128 * b + 128]

        sweep(db_ref, last)

    after = coarse(grow_ref[...].reshape(GOALS * CROWS, 128))
    wide = prolong_cols(after)
    spread = spread_of(iota((ROWS, 2 * CROWS), 0) + HALO)
    for g in range(GOALS):
        add = prolong_rows(wide[g * CROWS : (g + 1) * CROWS], spread)
        for b in tiles:
            o = one_zero(nat_ref[b, HALO : HALO + ROWS, :] > 0.0)
            finish(g, b, y_ref[g, b, HALO : HALO + ROWS, :] + o * add[:, 128 * b : 128 * b + 128])


def scratch_of(width):
    padded = pltpu.VMEM((STEPS + 2, 8, width), F32)
    plain = pltpu.VMEM((STEPS, 8, width), F32)
    return [
        pltpu.VMEM((width // 128, WIDE, 128), F32), padded, padded, plain, plain, padded, plain, plain, padded, padded, plain,
        plain, pltpu.VMEM((GOALS, width // 128, WIDE, 128), F32), plain, pltpu.VMEM((GOALS, CROWS, 128), F32),
    ]


def starts_early():
    return lax.axis_index("gy") == 8


def tile_of(src_ref, top_ref, bottom_ref, q, lo):
    if q < HALO // 8:
        return top_ref[8 * q : 8 * q + 8, lo : lo + 128]
    if q >= (HALO + ROWS) // 8:
        at = 8 * q - HALO - ROWS
        return bottom_ref[at : at + 8, lo : lo + 128]
    at = 8 * q - HALO
    return src_ref[at : at + 8, lo : lo + 128]


def do_tile(src_ref, top_ref, bottom_ref, rows_ref, cols_ref, part_ref, fringe_exits_ref, exits_ref, nat_ref, scratch):
    mark_exits(rows_ref, cols_ref, exits_ref, fringe_exits_ref)
    for b in range(COLS // 128):
        at = slice(128 * b, 128 * b + 128)
        nat_ref[b, 0:HALO, :] = top_ref[:, at]
        nat_ref[b, HALO : HALO + ROWS, :] = src_ref[:, at]
        nat_ref[b, HALO + ROWS : WIDE, :] = bottom_ref[:, at]

    def finish(g, b, x):
        part_ref[g, :, 128 * b : 128 * b + 128] = x

    run_cycles(COLS, lambda lane: lane, nat_ref, exits_ref, scratch, finish)


def early_kernel(
    src_ref, inner_ref, outer_ref, rows_ref, cols_ref,
    left_ref, right_ref, top_ref, bottom_ref, part_ref, fringe_exits_ref, exits_ref, nat_ref, *scratch,
):
    even = lax.rem(lax.axis_index("gx"), 2) == 0
    top_ref[...] = jnp.where(even, outer_ref[...], inner_ref[...])
    bottom_ref[...] = jnp.where(even, inner_ref[...], outer_ref[...])

    lane = iota((8, 128), 1)
    for b in range(STRIP // 128):
        left = jnp.zeros((8, 128), F32)
        right = jnp.zeros((8, 128), F32)
        for m in range(8):
            q = 8 * b + m
            if q >= STEPS:
                break
            here = (lane >= HALO * m) & (lane < HALO * (m + 1))
            first = tile_of(src_ref, top_ref, bottom_ref, q, 0)
            last = tile_of(src_ref, top_ref, bottom_ref, q, COLS - 128)
            left = jnp.where(here, pltpu.roll(first, HALO * m, 1), left)
            right = jnp.where(here, pltpu.roll(last, (HALO * m + HALO) % 128, 1), right)
        left_ref[:, 128 * b : 128 * b + 128] = left
        right_ref[:, 128 * b : 128 * b + 128] = right

    @pl.when(starts_early())
    def _():
        do_tile(src_ref, top_ref, bottom_ref, rows_ref, cols_ref, part_ref, fringe_exits_ref, exits_ref, nat_ref, scratch)


def late_kernel(
    src_ref, top_ref, bottom_ref, rows_ref, cols_ref, part_ref, fringe_exits_ref, exits_ref, nat_ref, *scratch
):
    @pl.when(jnp.logical_not(starts_early()))
    def _():
        do_tile(src_ref, top_ref, bottom_ref, rows_ref, cols_ref, part_ref, fringe_exits_ref, exits_ref, nat_ref, scratch)


STRIPS = [jax.ShapeDtypeStruct((8, STRIP), F32)] * 2 + [jax.ShapeDtypeStruct((HALO, COLS), F32)] * 2
PARTS = [jax.ShapeDtypeStruct((GOALS, ROWS, COLS), F32), jax.ShapeDtypeStruct((GOALS, WIDE, FRINGE), F32)]


def whole(count):
    return [pl.BlockSpec(memory_space=pltpu.VMEM)] * count


def call(kernel, outs, width, *args):
    exits = [pltpu.VMEM((GOALS, WIDE, width), F32)]
    return pl.pallas_call(
        kernel,
        out_shape=outs,
        in_specs=whole(len(args)),
        out_specs=whole(len(outs)),
        scratch_shapes=exits + scratch_of(width),
        compiler_params=pltpu.CompilerParams(vmem_limit_bytes=16 * 2**20),
        cost_estimate=pl.CostEstimate(flops=10**7, bytes_accessed=2**20, transcendentals=0),
    )(*args)


def fringe_kernel(
    src_ref, top_ref, bottom_ref, from_left_ref, from_right_ref, part_a_ref, exits_a_ref, part_b_ref, exits_b_ref, out_ref,
    exits_ref, nat_ref, *scratch,
):
    early = starts_early()
    lane = iota((8, 128), 1)
    half = FRINGE // 2
    for q in range(STEPS):
        b, m = divmod(q, 8)
        at = slice(128 * b, 128 * b + 128)
        behind = pltpu.roll(from_left_ref[:, at], (128 - HALO * m) % 128, 1)
        ahead = pltpu.roll(from_right_ref[:, at], (128 - HALO - HALO * m) % 128, 1)
        first = pltpu.roll(tile_of(src_ref, top_ref, bottom_ref, q, 0), HALO, 1)
        last = pltpu.roll(tile_of(src_ref, top_ref, bottom_ref, q, COLS - 128), 128 - HALO, 1)
        right = jnp.where(lane < 128 - HALO, last, ahead)
        nat_ref[0, 8 * q : 8 * q + 8, :] = jnp.where(lane < HALO, behind, jnp.where(lane < half, first, right))

    exits_ref[...] = jnp.where(early, exits_a_ref[...], exits_b_ref[...])
    lanes = iota((ROWS, 128), 1)

    def column(lane):
        return jnp.where(lane < half // 4, lane - HALO // 4, lane + (COLS + HALO - FRINGE) // 4)

    def finish(g, b, x):
        first = pltpu.roll(x, 128 - HALO, 1)
        last = pltpu.roll(x, HALO, 1)
        part = jnp.where(early, part_a_ref[g], part_b_ref[g])
        out_ref[g, :, 0:128] = jnp.where(lanes < HALO, first, part[:, 0:128])
        out_ref[g, :, 128:256] = jnp.where(lanes >= 128 - HALO, last, part[:, 128:256])

    run_cycles(FRINGE, column, nat_ref, exits_ref, scratch, finish)


def per_device(obstacles, load, exit_rows, exit_cols):
    gx = lax.axis_index("gx")
    nx, ny = lax.axis_size("gx"), lax.axis_size("gy")
    even = lax.rem(gx, 2) == 0
    source = jnp.where(obstacles == 0, load, 0.0)
    first, last = source[:HALO], source[ROWS - HALO :]
    got_inner = lax.ppermute(jnp.where(even, last, first), "gx", [(i, i ^ 1) for i in range(nx)])
    outer = [(i, ((i + 1) ^ 1) - 1) for i in range(1, nx - 1)]
    got_outer = lax.ppermute(jnp.where(even, first, last), "gx", outer)
    left, right, top, bottom, part_a, exits_a = call(
        early_kernel, STRIPS + PARTS, COLS, source, got_inner, got_outer, exit_rows, exit_cols
    )
    from_left = lax.ppermute(right, "gy", [(i, i + 1) for i in range(ny - 1)])
    from_right = lax.ppermute(left, "gy", [(i + 1, i) for i in range(ny - 1)])
    part_b, exits_b = call(late_kernel, PARTS, COLS, source, top, bottom, exit_rows, exit_cols)
    (out,) = call(
        fringe_kernel, PARTS[:1], FRINGE,
        source, top, bottom, from_left, from_right, part_a, exits_a, part_b, exits_b,
    )
    return out


def solution(mesh):
    in_specs = (P("gx", "gy"), P("gx", "gy"), P(), P())
    out_specs = P(None, "gx", "gy")
    return jax.shard_map(
        per_device, mesh=mesh, in_specs=in_specs, out_specs=out_specs, check_vma=False
    )
```

time: 32.1 us -> 27.4 us (0.85)
  the two profiles are of different devices: /device:TPU:31 before, /device:TPU:30 now
where the time goes in v3:
time: 27.4 us; the launch traced here: 27.1 us
  starting transfers between devices  16.4 us (60%)
  Pallas kernels  7.42 us (27%)
  waiting for transfers between devices  2.16 us (8%)
  other arithmetic  1.02 us (4%)
    ppermute x1, starting transfers between devices, per_device(): from_right = lax.ppermute(left, 'gy', [(i + 1, i) for i in range(ny - 1)])  7.54 us
    pallas_call x3, Pallas kernels, call(): pl.pallas_call(kernel, out_shape=outs, in_specs=whole(len(args)), out_spe...  7.42 us
    ppermute x1, starting transfers between devices, per_device(): lax.ppermute(jnp.where(even, last, first), 'gx', [(i, i ^ 1) for i in ran...  4.81 us
    ppermute x1, starting transfers between devices, per_device(): got_outer = lax.ppermute(jnp.where(even, first, last), 'gx', outer)  2.18 us
    ppermute x1, starting transfers between devices, per_device(): from_left = lax.ppermute(right, 'gy', [(i, i + 1) for i in range(ny - 1)])  1.92 us
    ppermute x1, waiting for transfers between devices, per_device(): from_right = lax.ppermute(left, 'gy', [(i + 1, i) for i in range(ny - 1)])  1.35 us
    select_n x1, other arithmetic, per_device(): source = jnp.where(obstacles == 0, load, 0.0)  1.02 us
    ppermute x1, waiting for transfers between devices, per_device(): lax.ppermute(jnp.where(even, last, first), 'gx', [(i, i ^ 1) for i in ran...  0.81 us
  transfers between devices with their start and end apart: 4, of which 2 were waited for; matrix products, arithmetic and copies ran while one was open for 0% of the time, Pallas kernels for 0%

profile of v3, /device:TPU:30, one launch (start us, length us, event | category | flops | bytes accessed | tf_op | source)
XLA Modules:
  0.0 27.1 jit_solution(6505586703787097609)
XLA Ops:
  0.0 0.0 copy-start.1
  0.0 1.0 %compare_select_fusion.src_ref = f32[128,256]{1,0:T(8,128)S(1)} fusion(f32[128,256]{1,0:T(8,128)} %param.5, s32[128,256]{1,0:T(8,128)} %param.4), kind=kLoop, calls=%fused_computation | loop fusion | flops 65536 | bytes 393216 | tf_op jit(solution)/shard_map/jit(_where)/select_n | solution.py:401
  1.0 0.0 copy-start
  1.0 2.2 %collective-permute-start.1 = (f32[16,256]{1,0:T(8,128)S(1)}, f32[16,256]{1,0:T(8,128)S(1)}, u32[]{:S(2)}, u32[]{:S(2)}) collective-permute-start(f32[16,256]{1,0:T(8,128)S(1)} %get-tuple-element.21), channel_id=1, source_target_pairs={{16,32},{32,16},{48,64},{64,48},{80,96},{96,80},{112,128},{128,112... | collective-permute-start | bytes 49160 | tf_op jit(solution)/shard_map/ppermute | solution.py:405
  3.2 4.8 %collective-permute-start = (f32[16,256]{1,0:T(8,128)S(1)}, f32[16,256]{1,0:T(8,128)S(1)}, u32[]{:S(2)}, u32[]{:S(2)}) collective-permute-start(f32[16,256]{1,0:T(8,128)S(1)} %get-tuple-element.22), channel_id=1, source_target_pairs={{0,16},{16,0},{32,48},{48,32},{64,80},{80,64},{96,112},{112,96},{1... | collective-permute-start | bytes 49160 | tf_op jit(solution)/shard_map/ppermute | solution.py:403
  8.0 0.0 collective-permute-done.1.outer_ref
  8.1 0.8 %collective-permute-done.inner_ref = f32[16,256]{1,0:T(8,128)S(1)} collective-permute-done((f32[16,256]{1,0:T(8,128)S(1)}, f32[16,256]{1,0:T(8,128)S(1)}, u32[]{:S(2)}, u32[]{:S(2)}) %collective-permute-start) | collective-permute-done | bytes 16416 | tf_op jit(solution)/shard_map/ppermute | solution.py:403
  8.9 0.0 copy-done.1
  8.9 0.0 copy-done
  8.9 4.3 %shard_map.46 = (f32[8,384]{1,0:T(8,128)S(1)}, f32[8,384]{1,0:T(8,128)S(1)}, f32[16,256]{1,0:T(8,128)S(1)}, f32[16,256]{1,0:T(8,128)S(1)}, f32[4,128,256]{2,1,0:T(8,128)S(1)}, /*index=5*/f32[4,160,128]{2,1,0:T(8,128)S(1)}) custom-call(f32[128,256]{1,0:T(8,128)S(1)} %compare_select_fusion.src_ref, f32[16,256]{1,0:T(8,128)S(1)} %collective-permute-done.inner_ref, ...), custom_call_target="tpu_custom_call" | custom-call | flops 10000000 | bytes 1048576 | tf_op jit(solution)/shard_map/pallas_call | solution.py:353
  13.2 1.9 %collective-permute-start.2 = (f32[8,384]{1,0:T(8,128)S(1)}, f32[8,384]{1,0:T(8,128)S(1)}, u32[]{:S(2)}, u32[]{:S(2)}) collective-permute-start(f32[8,384]{1,0:T(8,128)S(1)} %get-tuple-element.15), channel_id=1, source_target_pairs={{0,1},{1,2},{2,3},{3,4},{4,5},{5,6},{6,7},{7,8},{8,9},{9,10},{10,1... | collective-permute-start | bytes 36872 | tf_op jit(solution)/shard_map/ppermute | solution.py:409
  15.1 7.5 %collective-permute-start.3 = (f32[8,384]{1,0:T(8,128)S(1)}, f32[8,384]{1,0:T(8,128)S(1)}, u32[]{:S(2)}, u32[]{:S(2)}) collective-permute-start(f32[8,384]{1,0:T(8,128)S(1)} %get-tuple-element.16), channel_id=1, source_target_pairs={{1,0},{2,1},{3,2},{4,3},{5,4},{6,5},{7,6},{8,7},{9,8},{10,9},{11,1... | collective-permute-start | bytes 36872 | tf_op jit(solution)/shard_map/ppermute | solution.py:410
  22.6 0.0 collective-permute-done.2.from_left_ref
  22.7 1.4 %collective-permute-done.3.from_right_ref = f32[8,384]{1,0:T(8,128)S(1)} collective-permute-done((f32[8,384]{1,0:T(8,128)S(1)}, f32[8,384]{1,0:T(8,128)S(1)}, u32[]{:S(2)}, u32[]{:S(2)}) %collective-permute-start.3) | collective-permute-done | bytes 12320 | tf_op jit(solution)/shard_map/ppermute | solution.py:410
  24.0 3.1 %shard_map.48 = f32[4,128,256]{2,1,0:T(8,128)} custom-call(f32[128,256]{1,0:T(8,128)S(1)} %compare_select_fusion.src_ref, f32[16,256]{1,0:T(8,128)S(1)} %get-tuple-element.13.top_ref, f32[16,256]{1,0:T(8,128)S(1)} %get-tuple-element.14.bottom_ref, f32[8,384]{1,0:T(8,128)S(1)} %collective-permute-done.2.from_left_ref, ...), custom_call_target="tpu_custom_call" | custom-call | flops 10000000 | bytes 1048576 | tf_op jit(solution)/shard_map/pallas_call | solution.py:353
  (2 shorter events, 0.0 us)
Async XLA Ops:
  0.0 8.9 %copy-start.1 = (s32[4,4096]{1,0:T(4,128)S(1)}, s32[4,4096]{1,0:T(4,128)}, u32[]{:S(2)}) copy-start(s32[4,4096]{1,0:T(4,128)} %cols_ref.3) | copy-start | bytes 196612
  1.0 7.8 %copy-start = (s32[4,4096]{1,0:T(4,128)S(1)}, s32[4,4096]{1,0:T(4,128)}, u32[]{:S(2)}) copy-start(s32[4,4096]{1,0:T(4,128)} %rows_ref.3) | copy-start | bytes 196612
  1.0 7.0 %collective-permute-start.1 = (f32[16,256]{1,0:T(8,128)S(1)}, f32[16,256]{1,0:T(8,128)S(1)}, u32[]{:S(2)}, u32[]{:S(2)}) collective-permute-start(f32[16,256]{1,0:T(8,128)S(1)} %get-tuple-element.21), channel_id=1, source_target_pairs={{16,32},{32,16},{48,64},{64,48},{80,96},{96,80},{112,128},{128,112... | collective-permute-start | bytes 49160 | tf_op jit(solution)/shard_map/ppermute | solution.py:405
  3.2 5.6 %collective-permute-start = (f32[16,256]{1,0:T(8,128)S(1)}, f32[16,256]{1,0:T(8,128)S(1)}, u32[]{:S(2)}, u32[]{:S(2)}) collective-permute-start(f32[16,256]{1,0:T(8,128)S(1)} %get-tuple-element.22), channel_id=1, source_target_pairs={{0,16},{16,0},{32,48},{48,32},{64,80},{80,64},{96,112},{112,96},{1... | collective-permute-start | bytes 49160 | tf_op jit(solution)/shard_map/ppermute | solution.py:403
  13.2 9.5 %collective-permute-start.2 = (f32[8,384]{1,0:T(8,128)S(1)}, f32[8,384]{1,0:T(8,128)S(1)}, u32[]{:S(2)}, u32[]{:S(2)}) collective-permute-start(f32[8,384]{1,0:T(8,128)S(1)} %get-tuple-element.15), channel_id=1, source_target_pairs={{0,1},{1,2},{2,3},{3,4},{4,5},{5,6},{6,7},{7,8},{8,9},{9,10},{10,1... | collective-permute-start | bytes 36872 | tf_op jit(solution)/shard_map/ppermute | solution.py:409
  15.1 8.9 %collective-permute-start.3 = (f32[8,384]{1,0:T(8,128)S(1)}, f32[8,384]{1,0:T(8,128)S(1)}, u32[]{:S(2)}, u32[]{:S(2)}) collective-permute-start(f32[8,384]{1,0:T(8,128)S(1)} %get-tuple-element.16), channel_id=1, source_target_pairs={{1,0},{2,1},{3,2},{4,3},{5,4},{6,5},{7,6},{8,7},{9,8},{10,9},{11,1... | collective-permute-start | bytes 36872 | tf_op jit(solution)/shard_map/ppermute | solution.py:410
